TPU v7x, 32 devices: a whole 2x2x4 slice. The times are simulated.
32 devices in a mesh: gx: 16 (over z, x, core), gy: 2 (over y).
Axes of the slice: x: 2, y: 2, z: 4, core: 2. Of those that a mesh axis runs over, the one named last changes fastest.
Arguments:
- field: bfloat16 [512, 128, 512], P('gx', 'gy'), may hold values from -6 to 6
- perm_class: int32 [512, 4096], P('gx', 'gy'), may hold values from 0 to 7
- perm_table: float32 [8], replicated, may hold values from 0.05 to 0.5
- forcing: float32 [512, 4096], P('gx', 'gy'), may hold values from -6 to 6
- spec_weight: bfloat16 [2, 16, 16, 16, 16], replicated, may hold values from -1 to 1
- mix_weight: bfloat16 [16, 16], replicated, may hold values from -1.5 to 1.5
- proj: float32 [16], replicated, may hold values from -1.5 to 1.5
Outputs:
- residual: float32 [512, 4096], P('gx', 'gy')
- grad_field: bfloat16 [512, 128, 512], P('gx', 'gy')
- spec_grad: float32 [2, 16, 16, 16, 16], replicated
All inputs are finite; a program needn't handle non-finite values.
Results may differ from a plain program's by a relative error of at most 0.015.
Values may be sent and summed in bfloat16 or wider, within the bound.
A program may use at most 128 MiB of HBM per device.

v0:
```python
import math

import jax
import jax.numpy as jnp
from jax import lax
from jax.sharding import PartitionSpec as P

C = 16
KX = 16
KY = 16
CLASSES = 8


HIGHEST = lax.Precision.HIGHEST
ROOT_HALF = 0.7071067811865476
INV_ROOT_TWO_PI = 0.3989422804014327


def extended(block, sides, width):
    for axis, dim in sides:
        count = lax.axis_size(axis)
        forward = [(i, i + 1) for i in range(count - 1)]
        backward = [(target, source) for source, target in forward]
        low = lax.ppermute(
            lax.slice_in_dim(block, block.shape[dim] - width, None, axis=dim), axis, forward
        )
        high = lax.ppermute(lax.slice_in_dim(block, 0, width, axis=dim), axis, backward)
        block = jnp.concatenate([low, block, high], axis=dim)
    return block


def contract(form, left, right):
    return jnp.einsum(form, left, right, precision=HIGHEST)


def angle_tables(positions, length, count, scale):
    frequencies = jnp.arange(count, dtype=jnp.int32) - count // 2
    turns = positions[:, None] * frequencies[None, :] % length
    angle = turns.astype(jnp.float32) * (2.0 * math.pi / length)
    return (jnp.cos(angle) * scale, jnp.sin(angle) * scale)


def x_table(positions, length, scale):
    cosine, sine = angle_tables(positions, length, KX, scale)
    return jnp.concatenate([cosine, -sine], axis=1).astype(jnp.bfloat16)


def y_tables(length):
    positions = jnp.arange(length, dtype=jnp.int32)
    forward_cos, forward_sin = angle_tables(positions, length, KY, 1.0 / math.sqrt(length))
    inverse_cos, inverse_sin = angle_tables(positions, length, KY, 1.0 / math.sqrt(KY))
    return (forward_cos, forward_sin, inverse_cos, inverse_sin)


def y_forward(part, forward_cos, forward_sin):
    real_part = part[..., 0, :, :, :]
    imaginary = part[..., 1, :, :, :]
    form = "...ayc,yb->...abc"
    real_result = contract(form, real_part, forward_cos) + contract(form, imaginary, forward_sin)
    imag_result = contract(form, imaginary, forward_cos) - contract(form, real_part, forward_sin)
    return jnp.stack([real_result, imag_result], axis=-4)


def mix_modes(coefficients, weight_real, weight_imaginary):
    real_part = coefficients[..., 0, :, :, :]
    imaginary = coefficients[..., 1, :, :, :]
    form = "...abc,abco->...abo"
    real_result = contract(form, real_part, weight_real) - contract(
        form, imaginary, weight_imaginary
    )
    imag_result = contract(form, real_part, weight_imaginary) + contract(
        form, imaginary, weight_real
    )
    return jnp.stack([real_result, imag_result], axis=-4)


def y_inverse(mixed, inverse_cos, inverse_sin):
    real_part = mixed[..., 0, :, :, :]
    imaginary = mixed[..., 1, :, :, :]
    form = "...abc,yb->...ayc"
    real_result = contract(form, real_part, inverse_cos) - contract(form, imaginary, inverse_sin)
    imag_result = contract(form, real_part, inverse_sin) + contract(form, imaginary, inverse_cos)
    return jnp.stack([real_result, imag_result], axis=-4)


def y_inverse_adjoint(grad_back, inverse_cos, inverse_sin):
    real_part = grad_back[..., 0, :, :, :]
    imaginary = grad_back[..., 1, :, :, :]
    form = "...ayc,yb->...abc"
    real_result = contract(form, real_part, inverse_cos) + contract(form, imaginary, inverse_sin)
    imag_result = contract(form, imaginary, inverse_cos) - contract(form, real_part, inverse_sin)
    return jnp.stack([real_result, imag_result], axis=-4)


def mix_adjoint(coefficients, grad_out, weight_real, weight_imaginary):
    coef_real = coefficients[..., 0, :, :, :]
    coef_imaginary = coefficients[..., 1, :, :, :]
    grad_real = grad_out[..., 0, :, :, :]
    grad_imaginary = grad_out[..., 1, :, :, :]
    form = "...abo,abco->...abc"
    input_real = contract(form, grad_real, weight_real) + contract(
        form, grad_imaginary, weight_imaginary
    )
    input_imaginary = contract(form, grad_imaginary, weight_real) - contract(
        form, grad_real, weight_imaginary
    )
    outer = "...abc,...abo->abco"
    weight_grad_real = contract(outer, coef_real, grad_real) + contract(
        outer, coef_imaginary, grad_imaginary
    )
    weight_grad_imaginary = contract(outer, coef_real, grad_imaginary) - contract(
        outer, coef_imaginary, grad_real
    )
    return (
        jnp.stack([input_real, input_imaginary], axis=-4),
        jnp.stack([weight_grad_real, weight_grad_imaginary], axis=0),
    )


def y_forward_adjoint(grad_coef, forward_cos, forward_sin):
    real_part = grad_coef[..., 0, :, :, :]
    imaginary = grad_coef[..., 1, :, :, :]
    form = "...abc,yb->...ayc"
    real_result = contract(form, real_part, forward_cos) - contract(form, imaginary, forward_sin)
    imag_result = contract(form, real_part, forward_sin) + contract(form, imaginary, forward_cos)
    return jnp.stack([real_result, imag_result], axis=-4)


def gelu_value(preact):
    return 0.5 * preact * (1.0 + lax.erf(preact * ROOT_HALF))


def gelu_slope(preact):
    return (
        0.5 * (1.0 + lax.erf(preact * ROOT_HALF))
        + preact * jnp.exp(-0.5 * preact * preact) * INV_ROOT_TWO_PI
    )


def apply_operator(values, permeability):
    centre_value = values[1:-1, 1:-1, 1:-1]
    centre_perm = permeability[1:-1, 1:-1, 1:-1]
    total = jnp.zeros_like(centre_value)
    for axis in range(3):
        for offset in (0, 2):
            index = [slice(1, -1), slice(1, -1), slice(1, -1)]
            index[axis] = slice(offset, offset + centre_value.shape[axis])
            neighbour_value = values[tuple(index)]
            neighbour_perm = permeability[tuple(index)]
            total = total + 0.5 * (centre_perm + neighbour_perm) * (centre_value - neighbour_value)
    return total


def to_coefficients(data, scale):
    rows_x = data.shape[0]
    rows_y = data.shape[1]
    depth = data.shape[2] // C
    span = rows_x * lax.axis_size("gx")
    owned = depth // lax.axis_size("gx")
    table = x_table(jnp.arange(span, dtype=jnp.int32), span, scale)
    slab = lax.all_to_all(data, "gx", split_axis=2, concat_axis=0, tiled=True)
    count = slab.shape[1]
    layered = slab.reshape(span, count, owned, C)
    result = jnp.einsum("xj,xyzc->zjyc", table, layered, preferred_element_type=jnp.float32)
    return result.reshape(owned, 2 * KX, rows_y * C)


def from_coefficients(values, rows_x, scale):
    owned = values.shape[0]
    rows_y = values.shape[2] // C
    span = rows_x * lax.axis_size("gx")
    table = x_table(jnp.arange(span, dtype=jnp.int32), span, scale)
    layered = values.reshape(owned, 2 * KX, rows_y, C)
    spread = jnp.einsum("xj,zjyc->xyzc", table, layered, preferred_element_type=jnp.float32)
    spread = spread.astype(jnp.bfloat16).reshape(span, rows_y, owned * C)
    return lax.all_to_all(spread, "gx", split_axis=0, concat_axis=2, tiled=True)


def to_pencil(values):
    owned = values.shape[0]
    split = values.reshape(owned, 2, KX, values.shape[2])
    moved = lax.all_to_all(split, "gy", split_axis=2, concat_axis=3, tiled=True)
    return moved.reshape(owned, 2, moved.shape[2], -1, C)


def from_pencil(values):
    owned = values.shape[0]
    block = values.shape[2]
    flat = values.reshape(owned, 2, block, values.shape[3] * C)
    moved = lax.all_to_all(flat, "gy", split_axis=3, concat_axis=2, tiled=True)
    return moved.reshape(owned, 2 * KX, moved.shape[3])


def shards(field, perm_class, perm_table, forcing, spec_weight, mix_weight, proj):
    rows_x = field.shape[0]
    rows_y = field.shape[1]
    width = field.shape[2]
    depth = width // C
    span_x = rows_x * lax.axis_size("gx")
    span_y = rows_y * lax.axis_size("gy")
    block = KX // lax.axis_size("gy")
    forward_cos, forward_sin, inverse_cos, inverse_sin = y_tables(span_y)
    first_mode = lax.axis_index("gy") * block
    weights = lax.dynamic_slice_in_dim(spec_weight, first_mode, block, 1).astype(jnp.float32)
    weight_real = weights[0]
    weight_imaginary = weights[1]
    forward_scale = 1.0 / math.sqrt(span_x)
    inverse_scale = 1.0 / math.sqrt(KX)
    partial_sums = to_coefficients(field, forward_scale)
    coefficients = y_forward(to_pencil(partial_sums), forward_cos, forward_sin)
    mixed = mix_modes(coefficients, weight_real, weight_imaginary)
    back = y_inverse(mixed, inverse_cos, inverse_sin).astype(jnp.bfloat16)
    spectral = from_coefficients(from_pencil(back), rows_x, inverse_scale)
    volume = field.reshape(rows_x, rows_y, depth, C)
    local = jnp.einsum("xyzd,dc->xyzc", volume, mix_weight, preferred_element_type=jnp.float32)
    preact = spectral.reshape(rows_x, rows_y, depth, C).astype(jnp.float32) + local
    pressure = jnp.sum(gelu_value(preact) * proj, axis=3)
    classes = perm_class.reshape(rows_x, rows_y, depth)
    permeability = jnp.zeros(classes.shape, jnp.float32)
    for level in range(CLASSES):
        permeability = permeability + jnp.where(classes == level, perm_table[level], 0.0)
    stacked = jnp.stack([pressure, permeability])
    padded = extended(stacked, (("gx", 1), ("gy", 2)), 1)
    padded = jnp.pad(padded, ((0, 0), (0, 0), (0, 0), (1, 1)))
    applied = apply_operator(padded[0], padded[1])
    residual = applied - forcing.reshape(rows_x, rows_y, depth)
    padded_residual = extended(residual, (("gx", 0), ("gy", 1)), 1)
    padded_residual = jnp.pad(padded_residual, ((0, 0), (0, 0), (1, 1)))
    grad_pressure = apply_operator(padded_residual, padded[1])
    grad_pre = (proj * grad_pressure[..., None] * gelu_slope(preact)).astype(jnp.bfloat16)
    flat_grad = grad_pre.reshape(rows_x, rows_y, width)
    grad_back = to_coefficients(flat_grad, inverse_scale)
    grad_out = y_inverse_adjoint(to_pencil(grad_back), inverse_cos, inverse_sin)
    grad_coef, grad_weight = mix_adjoint(coefficients, grad_out, weight_real, weight_imaginary)
    weight_total = lax.psum(grad_weight.astype(jnp.bfloat16), "gx").astype(jnp.float32)
    spec_grad = lax.all_gather(weight_total.astype(jnp.bfloat16), "gy", axis=1, tiled=True).astype(
        weight_total.dtype
    )
    grad_part = y_forward_adjoint(grad_coef, forward_cos, forward_sin).astype(jnp.bfloat16)
    grad_spec = from_coefficients(from_pencil(grad_part), rows_x, forward_scale)
    grad_local = jnp.einsum(
        "xyzc,dc->xyzd", grad_pre, mix_weight, preferred_element_type=jnp.float32
    )
    grad_field = (
        grad_spec.reshape(rows_x, rows_y, depth, C).astype(jnp.float32) + grad_local
    ).astype(jnp.bfloat16)
    return (
        residual.reshape(rows_x, rows_y * depth),
        grad_field.reshape(rows_x, rows_y, width),
        spec_grad,
    )


def solution(mesh):
    placed = (P("gx", "gy", None), P("gx", "gy"), P(), P("gx", "gy"), P(), P(), P())
    return jax.shard_map(
        shards,
        mesh=mesh,
        in_specs=placed,
        out_specs=(P("gx", "gy"), P("gx", "gy", None), P()),
        check_vma=False,
    )
```

profile of v0, /device:TPU:0, one launch (start us, length us, event | category | flops | bytes accessed | tf_op | source)
XLA Modules:
  0.0 657.4 jit_solution(12925757472292514244)
XLA Ops:
  7.2 7.6 %copy.383 = bf16[32,64,512]{1,0,2:T(8,128)(2,1)} copy(bf16[32,64,512]{2,1,0:T(8,128)(2,1)} %param.7) | data formatting | bytes 4194304 | tf_op args[0]
  14.7 7.5 %reshape.266 = bf16[16,2,32768]{2,1,0:T(2,128)(2,1)} reshape(bf16[512,32,64]{2,1,0:T(8,128)(2,1)} %bitcast.240) | data formatting | bytes 4194304
  22.2 7.4 %all-to-all-start = ((bf16[16,2,32768]{2,1,0:T(2,128)(2,1)}), bf16[16,2,32768]{2,1,0:T(2,128)(2,1)}, u32[]{:S(2)}, u32[]{:S(2)}) async-start(bf16[16,2,32768]{2,1,0:T(2,128)(2,1)} %reshape.266), calls=%async_computation | async-start | bytes 4194304 | tf_op jit(solution)/shard_map/all_to_all | solution.py:161
  29.9 40.9 %all-to-all-done = bf16[16,2,32768]{2,1,0:T(2,128)(2,1)} async-done(((bf16[16,2,32768]{2,1,0:T(2,128)(2,1)}), bf16[16,2,32768]{2,1,0:T(2,128)(2,1)}, u32[]{:S(2)}, u32[]{:S(2)}) %all-to-all-start) | async-done | bytes 2097184 | tf_op jit(solution)/shard_map/all_to_all | solution.py:161
  70.8 7.4 %reshape.267 = bf16[512,32,64]{2,1,0:T(8,128)(2,1)} reshape(bf16[16,2,32768]{2,1,0:T(2,128)(2,1)} %all-to-all-done) | data formatting | bytes 4194304
  93.2 6.3 all-to-all-done.1
  120.5 7.2 %all_to_all.108 = bf16[2,2,16384]{2,1,0:T(2,128)(2,1)S(1)} all-to-all(bf16[2,2,16384]{2,1,0:T(2,128)(2,1)S(1)} %reshape.268), channel_id=1, replica_groups=mesh['gx'=16,'gy'=2] {'gy'}, dimensions={0} | all-to-all | bytes 262144 | tf_op jit(solution)/shard_map/all_to_all | solution.py:190
  139.0 8.8 %copy.407 = bf16[512,64,32]{1,2,0:T(8,128)(2,1)} copy(bf16[512,64,32]{0,2,1:T(8,128)(2,1)} %bitcast.249) | data formatting | bytes 4194304 | tf_op jit(solution)/shard_map/reshape | solution.py:175
  147.8 7.5 %reshape.270 = bf16[16,2,32768]{2,1,0:T(2,128)(2,1)} reshape(bf16[512,32,64]{2,1,0:T(8,128)(2,1)} %bitcast.238) | data formatting | bytes 4194304
  155.3 10.8 %all-to-all-start.3 = ((bf16[16,2,32768]{2,1,0:T(2,128)(2,1)}), bf16[16,2,32768]{2,1,0:T(2,128)(2,1)}, u32[]{:S(2)}, u32[]{:S(2)}) async-start(bf16[16,2,32768]{2,1,0:T(2,128)(2,1)} %reshape.270), calls=%async_computation.3 | async-start | bytes 4194304 | tf_op jit(solution)/shard_map/all_to_all | solution.py:176
  166.1 4.9 copy.409
  171.7 5.4 add_add_fusion
  180.0 27.3 %all-to-all-done.3 = bf16[16,2,32768]{2,1,0:T(2,128)(2,1)} async-done(((bf16[16,2,32768]{2,1,0:T(2,128)(2,1)}), bf16[16,2,32768]{2,1,0:T(2,128)(2,1)}, u32[]{:S(2)}, u32[]{:S(2)}) %all-to-all-start.3) | async-done | bytes 2097184 | tf_op jit(solution)/shard_map/all_to_all | solution.py:176
  207.2 7.4 %reshape.271 = bf16[512,32,64]{2,1,0:T(8,128)(2,1)} reshape(bf16[16,2,32768]{2,1,0:T(2,128)(2,1)} %all-to-all-done.3) | data formatting | bytes 4194304
  219.5 7.6 %multiply_reduce_fusion = (f32[32,64,32]{1,2,0:T(8,128)S(1)}, f32[32,64,32,16]{1,3,2,0:T(8,128)}) fusion(f32[16]{0:T(128)S(1)} %copy-done.13, f32[32,64,32,16]{1,3,2,0:T(8,128)S(1)} %bitcast.232, bf16[32,64,32,16]{1,3,2,0:T(8,128)(2,1)} %bitcast.234, bf16[16,16]{1,0:T(8,128)(2,1)S(1)} %copy-done.12), kind=kOutput, calls=%fused_computation.10 | convolution fusion | flops 40828928 | bytes 10748480 | tf_op jit(solution)/shard_map/xyzd,dc->xyzc/dot_general | solution.py:215
  259.3 4.9 collective-permute-start.4
  271.6 5.7 collective-permute-start.6
  284.9 6.3 fusion.5
  295.9 7.5 %reshape.272 = bf16[16,2,32768]{2,1,0:T(2,128)(2,1)} reshape(bf16[512,32,64]{2,1,0:T(8,128)(2,1)} %bitcast.245) | data formatting | bytes 4194304
  303.4 62.9 %all_to_all.109 = bf16[16,2,32768]{2,1,0:T(2,128)(2,1)} all-to-all(bf16[16,2,32768]{2,1,0:T(2,128)(2,1)} %reshape.272), channel_id=1, replica_groups=mesh['gx'=16,'gy'=2] {'gx'}, dimensions={0} | all-to-all | bytes 4194304 | tf_op jit(solution)/shard_map/all_to_all | solution.py:161
  366.3 7.4 %reshape.273 = bf16[512,32,64]{2,1,0:T(8,128)(2,1)} reshape(bf16[16,2,32768]{2,1,0:T(2,128)(2,1)} %all_to_all.109) | data formatting | bytes 4194304
  373.6 5.9 copy.426
  379.6 6.8 %copy.427 = bf16[512,64,2,16]{0,3,2,1:T(8,128)(2,1)} copy(bf16[512,64,2,16]{1,3,2,0:T(8,128)(2,1)} %bitcast.244) | data formatting | bytes 4194304 | tf_op jit(solution)/shard_map/reshape | solution.py:163
  397.0 9.2 %all_to_all.110 = f32[2,2,16,1024]{3,1,0,2:T(2,128)S(1)} all-to-all(f32[2,2,16,1024]{3,1,0,2:T(2,128)S(1)} %copy.429), channel_id=1, replica_groups=mesh['gx'=16,'gy'=2] {'gy'}, dimensions={2} | all-to-all | bytes 524288 | tf_op jit(solution)/shard_map/all_to_all | solution.py:182
  435.0 7.0 %all_to_all.111 = bf16[2,2,16384]{2,1,0:T(2,128)(2,1)S(1)} all-to-all(bf16[2,2,16384]{2,1,0:T(2,128)(2,1)S(1)} %reshape.274), channel_id=1, replica_groups=mesh['gx'=16,'gy'=2] {'gy'}, dimensions={0} | all-to-all | bytes 262144 | tf_op jit(solution)/shard_map/all_to_all | solution.py:190
  455.5 8.8 %copy.448 = bf16[512,64,32]{1,2,0:T(8,128)(2,1)} copy(bf16[512,64,32]{0,2,1:T(8,128)(2,1)} %bitcast.250) | data formatting | bytes 4194304 | tf_op jit(solution)/shard_map/reshape | solution.py:175
  464.2 7.5 %reshape.276 = bf16[16,2,32768]{2,1,0:T(2,128)(2,1)} reshape(bf16[512,32,64]{2,1,0:T(8,128)(2,1)} %bitcast.239) | data formatting | bytes 4194304
  471.7 4.8 all-to-all-start.7
  489.2 106.6 %all-reduce.4.cloned.1.call-done = bf16[2,8,16,16,16]{4,3,2,1,0:T(8,128)(2,1)} async-done(((bf16[2,8,16,16,16]{4,3,2,1,0:T(8,128)(2,1)}), bf16[2,8,16,16,16]{4,3,2,1,0:T(8,128)(2,1)}) %all-reduce.4.cloned.1.call-update) | async-done | bytes 131088 | tf_op jit(solution)/shard_map/psum | solution.py:235
  595.8 25.4 %all_gather.3 = bf16[2,16,16,16,16]{4,3,2,1,0:T(8,128)(2,1)S(1)} all-gather(bf16[2,8,16,16,16]{4,3,2,1,0:T(8,128)(2,1)} %all-reduce.4.cloned.1.call-done), channel_id=1, replica_groups=mesh['gx'=16,'gy'=2] {'gy'}, dimensions={1}, use_global_device_ids=true | all-gather | bytes 393216 | tf_op jit(solution)/shard_map/all_gather | solution.py:236
  623.7 7.4 %reshape.277 = bf16[512,32,64]{2,1,0:T(8,128)(2,1)} reshape(bf16[16,2,32768]{2,1,0:T(2,128)(2,1)} %all-to-all-done.7) | data formatting | bytes 4194304
  631.2 6.6 %convert_bitcast_fusion = f32[32,64,16,32]{1,3,0,2:T(8,128)} fusion(bf16[16,32,64,32]{2,3,1,0:T(8,128)(2,1)} %bitcast.237), kind=kLoop, calls=%fused_computation.7 | loop fusion | flops 1048576 | bytes 6291456 | tf_op jit(solution)/shard_map/convert_element_type | solution.py:245
  (153 shorter events, 187.8 us)
Async XLA Ops:
  7.2 100.0 %copy-start = (bf16[2,16,16,16,16]{4,3,2,1,0:T(8,128)(2,1)S(1)}, bf16[2,16,16,16,16]{4,3,2,1,0:T(8,128)(2,1)}, u32[]{:S(2)}) copy-start(bf16[2,16,16,16,16]{4,3,2,1,0:T(8,128)(2,1)} %param.11) | copy-start | bytes 786436
  22.2 48.6 %all-to-all-start = ((bf16[16,2,32768]{2,1,0:T(2,128)(2,1)}), bf16[16,2,32768]{2,1,0:T(2,128)(2,1)}, u32[]{:S(2)}, u32[]{:S(2)}) async-start(bf16[16,2,32768]{2,1,0:T(2,128)(2,1)} %reshape.266), calls=%async_computation | async-start | bytes 4194304 | tf_op jit(solution)/shard_map/all_to_all | solution.py:161
  89.6 10.0 %all-to-all-start.1 = ((f32[2,2,16,1024]{3,1,0,2:T(2,128)}), f32[2,2,16,1024]{3,1,0,2:T(2,128)S(1)}, u32[]{:S(2)}, u32[]{:S(2)}) async-start(f32[2,2,16,1024]{3,1,0,2:T(2,128)} %copy.388), calls=%async_computation.1 | async-start | bytes 524288 | tf_op jit(solution)/shard_map/all_to_all | solution.py:182
  101.8 4.0 copy-start.4
  106.5 1.3 copy-start.7
  155.3 52.0 %all-to-all-start.3 = ((bf16[16,2,32768]{2,1,0:T(2,128)(2,1)}), bf16[16,2,32768]{2,1,0:T(2,128)(2,1)}, u32[]{:S(2)}, u32[]{:S(2)}) async-start(bf16[16,2,32768]{2,1,0:T(2,128)(2,1)} %reshape.270), calls=%async_computation.3 | async-start | bytes 4194304 | tf_op jit(solution)/shard_map/all_to_all | solution.py:176
  166.1 4.9 copy-start.11
  166.1 5.6 copy-start.10
  218.0 1.5 copy-start.12
  218.0 1.5 copy-start.13
  227.1 4.6 collective-permute-start.1
  228.4 4.2 collective-permute-start
  236.3 12.6 %collective-permute-start.3 = (f32[2,34,1,32]{1,3,2,0:T(8,128)S(1)}, f32[2,34,1,32]{1,3,2,0:T(8,128)S(1)}, u32[]{:S(2)}, u32[]{:S(2)}) collective-permute-start(f32[2,34,1,32]{1,3,2,0:T(8,128)S(1)} %copy.413), channel_id=1, source_target_pairs={{1,0},{3,2},{5,4},{7,6},{9,8},{11,10},{13,12},{15,14},{17,16},{19,... | collective-permute-start | bytes 26120 | tf_op jit(solution)/shard_map/ppermute | solution.py:27
  239.5 11.4 %collective-permute-start.2 = (f32[2,34,1,32]{1,3,2,0:T(8,128)S(1)}, f32[2,34,1,32]{1,3,2,0:T(8,128)S(1)}, u32[]{:S(2)}, u32[]{:S(2)}) collective-permute-start(f32[2,34,1,32]{1,3,2,0:T(8,128)S(1)} %copy.412), channel_id=1, source_target_pairs={{0,1},{2,3},{4,5},{6,7},{8,9},{10,11},{12,13},{14,15},{16,17},{18,... | collective-permute-start | bytes 26120 | tf_op jit(solution)/shard_map/ppermute | solution.py:24
  255.2 1.0 copy-start.9
  258.0 6.2 collective-permute-start.5
  259.3 5.7 collective-permute-start.4
  268.3 9.1 %collective-permute-start.7 = (f32[34,1,32]{0,2,1:T(8,128)}, f32[34,1,32]{0,2,1:T(8,128)}, u32[]{:S(2)}, u32[]{:S(2)}) collective-permute-start(f32[34,1,32]{0,2,1:T(8,128)} %copy.420), channel_id=1, source_target_pairs={{1,0},{3,2},{5,4},{7,6},{9,8},{11,10},{13,12},{15,14},{17,16},{19,... | collective-permute-start | bytes 13064 | tf_op jit(solution)/shard_map/ppermute | solution.py:27
  271.6 7.8 %collective-permute-start.6 = (f32[34,1,32]{0,2,1:T(8,128)}, f32[34,1,32]{0,2,1:T(8,128)}, u32[]{:S(2)}, u32[]{:S(2)}) collective-permute-start(f32[34,1,32]{0,2,1:T(8,128)} %copy.418), channel_id=1, source_target_pairs={{0,1},{2,3},{4,5},{6,7},{8,9},{10,11},{12,13},{14,15},{16,17},{18,... | collective-permute-start | bytes 13064 | tf_op jit(solution)/shard_map/ppermute | solution.py:24
  281.4 1.8 copy-start.5
  281.4 1.8 copy-start.6
  283.2 1.6 copy-start.14
  291.1 4.7 copy-start.1
  408.4 4.0 copy-start.3
  471.7 4.9 copy-start.8
  471.7 152.0 %all-to-all-start.7 = ((bf16[16,2,32768]{2,1,0:T(2,128)(2,1)}), bf16[16,2,32768]{2,1,0:T(2,128)(2,1)}, u32[]{:S(2)}, u32[]{:S(2)}) async-start(bf16[16,2,32768]{2,1,0:T(2,128)(2,1)} %reshape.276), calls=%async_computation.7 | async-start | bytes 4194304 | tf_op jit(solution)/shard_map/all_to_all | solution.py:176
  476.6 119.3 %all-reduce.4.cloned.1.call-start = ((), (), s32[]{:S(2)}) async-start(), calls=%async_computation.8 | async-start | bytes 2097152 | tf_op jit(solution)/shard_map/psum | solution.py:235
  637.8 4.6 copy-start.2
Sparse Core Ops, SparseCore 0:
  485.6 110.2 all-reduce.3
where the time goes:
time: 667 us; the launch traced here: 657 us
  local copies, waits for them, and re-layouts  216 us (32%)
  waiting for transfers between devices  183 us (27%)
  blocking collectives  112 us (17%)
  starting transfers between devices  50.4 us (8%)
  matrix products  47.9 us (7%)
  other arithmetic  33.3 us (5%)
  between operations  14.9 us (2%)
    psum x1, waiting for transfers between devices, shards(): lax.psum(grad_weight.astype(jnp.bfloat16), 'gx').astype(jnp.float32)  107 us
    unnamed x45, local copies, waits for them, and re-layouts  91.5 us
    all_to_all x1, blocking collectives, to_coefficients(): slab = lax.all_to_all(data, 'gx', split_axis=2, concat_axis=0, tiled=True)  62.9 us
    all_to_all x1, waiting for transfers between devices, to_coefficients(): slab = lax.all_to_all(data, 'gx', split_axis=2, concat_axis=0, tiled=True)  40.9 us
    dot_general x28, matrix products, contract(): return jnp.einsum(form, left, right, precision=HIGHEST)  29.5 us
    all_to_all x2, waiting for transfers between devices, from_coefficients(): return lax.all_to_all(spread, 'gx', split_axis=0, concat_axis=2, tiled=True)  27.3 us
    all_gather x1, blocking collectives, shards(): lax.all_gather(weight_total.astype(jnp.bfloat16), 'gy', axis=1, tiled=True)  25.4 us
    ppermute x4, starting transfers between devices, extended(): lax.ppermute(lax.slice_in_dim(block, block.shape[dim] - width, None, axis...  18.6 us
  transfers between devices with their start and end apart: 13, of which 6 were waited for; matrix products, arithmetic and copies ran while one was open for 6% of the time, Pallas kernels for 0%

commit v1 on v0

v1 whole, which is shorter than its diff:
```python
import functools
import math

import jax
import jax.numpy as jnp
import numpy as np
from jax import lax
from jax.experimental import pallas as pl
from jax.experimental.pallas import tpu as pltpu
from jax.sharding import PartitionSpec as P

C = 16
KX = 16
KY = 16
CLASSES = 8
LANES = 128
ROOT_HALF = 0.7071067811865476
INV_ROOT_TWO_PI = 0.3989422804014327
MESH = pl.DeviceIdType.MESH
F32 = jnp.float32
BF16 = jnp.bfloat16


def dot(left, right):
    return jnp.dot(left, right, preferred_element_type=F32)


def dot_first(left, right):
    return lax.dot_general(left, right, (((0,), (0,)), ((), ())), preferred_element_type=F32)


def split_dot(value, right):
    high = value.astype(BF16)
    low = (value - high.astype(F32)).astype(BF16)
    return dot(high, right) + dot(low, right)


def lane_iota(shape):
    return lax.broadcasted_iota(jnp.int32, shape, len(shape) - 1)


def group_roll(value, amount):
    if amount == 0:
        return value
    inside = lane_iota(value.shape) % C >= amount
    return jnp.where(
        inside, pltpu.roll(value, amount, 1), pltpu.roll(value, LANES - C + amount, 1)
    )


def kernel(
    gxn,
    gyn,
    owners,
    rows_x,
    rows_y,
    depth,
    field_ref,
    class_ref,
    table_ref,
    forcing_ref,
    x_ref,
    y_ref,
    weight_ref,
    mix_ref,
    mix_t_ref,
    proj_ref,
    sum_ref,
    spread_ref,
    residual_ref,
    grad_ref,
    spec_ref,
    fwd_ref,
    inv_ref,
    send_ref,
    recv_ref,
    out_ref,
    gout_ref,
    slope_ref,
    pre_ref,
    press_ref,
    coef_ref,
    x_send,
    x_recv,
    y_send,
    y_recv,
    send_sem,
    recv_sem,
    halo_send,
    halo_recv,
):
    n = gxn * gyn
    gx = lax.axis_index("gx")
    gy = lax.axis_index("gy")
    me = gx * gyn + gy
    apart = n // owners
    own = me // apart
    owner = me % apart == 0
    cells = rows_x * rows_y
    width = depth * C
    block = 2 * KX * KY // owners
    half = block // 2
    per = LANES // depth
    span = rows_y * depth
    columns = owners * block

    def if_owner(body):
        if apart == 1:
            body()
        else:
            pl.when(owner)(body)

    def place(index):
        return (index // gyn, index % gyn)

    barrier = pltpu.get_barrier_semaphore()

    def greet(k, carry):
        target = lax.rem(me + k, n)
        pl.semaphore_signal(barrier, inc=1, device_id=place(target), device_id_type=MESH)
        return carry

    lax.fori_loop(1, n, greet, 0)

    def fill(which, ref):
        def body(x, carry):
            first = x_ref[2 * which, pl.ds(x, 1), :]
            second = x_ref[2 * which + 1, pl.ds(x, 1), :]
            made = first * y_ref[2 * which] + second * y_ref[2 * which + 1]
            start = pl.multiple_of(x * rows_y, rows_y)
            ref[pl.ds(start, rows_y), :] = made.astype(BF16)
            return carry

        lax.fori_loop(0, rows_x, body, 0)

    fill(0, fwd_ref)
    pl.semaphore_wait(barrier, n - 1)

    classes = class_ref[...]
    perm = jnp.zeros(classes.shape, F32)
    for level in range(CLASSES):
        perm = jnp.where(classes == level, table_ref[level], perm)

    sides = (
        (gx > 0, (gx - 1, gy), x_send, x_recv, 0),
        (gx < gxn - 1, (gx + 1, gy), x_send, x_recv, 1),
        (gy > 0, (gx, gy - 1), y_send, y_recv, 0),
        (gy < gyn - 1, (gx, gy + 1), y_send, y_recv, 1),
    )

    def halo_copy(turn, side):
        _, target, source, landing, end = sides[side]
        return pltpu.make_async_remote_copy(
            src_ref=source.at[turn, end],
            dst_ref=landing.at[turn, 1 - end],
            send_sem=halo_send.at[turn, side],
            recv_sem=halo_recv.at[turn, side ^ 1],
            device_id=target,
            device_id_type=MESH,
        )

    def halo_start(turn, value):
        x_send[turn, 0] = value[0:1, :]
        x_send[turn, 1] = value[rows_x - 1 : rows_x, :]
        y_send[turn, 0] = value[:, 0:LANES]
        y_send[turn, 1] = value[:, span - LANES : span]
        for side in range(4):
            there, _, _, landing, end = sides[side]

            @pl.when(there)
            def _():
                halo_copy(turn, side).start()

            @pl.when(jnp.logical_not(there))
            def _():
                landing[turn, end] = jnp.zeros(landing.shape[2:], F32)

    def halo_wait(turn):
        for side in range(4):
            there, _, _, landing, end = sides[side]

            @pl.when(there)
            def _():
                copy = halo_copy(turn, side)
                copy.wait_send()
                pltpu.make_async_copy(
                    landing.at[turn, end], landing.at[turn, end], halo_recv.at[turn, side]
                ).wait()

    row = lax.broadcasted_iota(jnp.int32, (rows_x, span), 0)
    layer = lane_iota((rows_x, span)) % depth
    lane = lane_iota((rows_x, LANES))

    def neighbours(turn, value):
        below = jnp.where(row == 0, x_recv[turn, 0], pltpu.roll(value, 1, 0))
        above = jnp.where(row == rows_x - 1, x_recv[turn, 1], pltpu.roll(value, rows_x - 1, 0))
        moved = pltpu.roll(value, depth, 1)
        edge = jnp.where(lane < depth, pltpu.roll(y_recv[turn, 0], depth, 1), moved[:, :LANES])
        left = jnp.concatenate([edge, moved[:, LANES:]], axis=1)
        moved = pltpu.roll(value, span - depth, 1)
        edge = jnp.where(
            lane >= LANES - depth,
            pltpu.roll(y_recv[turn, 1], LANES - depth, 1),
            moved[:, span - LANES :],
        )
        right = jnp.concatenate([moved[:, : span - LANES], edge], axis=1)
        under = jnp.where(layer == 0, 0.0, pltpu.roll(value, 1, 1))
        over = jnp.where(layer == depth - 1, 0.0, pltpu.roll(value, span - 1, 1))
        return (below, above, left, right, under, over)

    halo_start(0, perm)

    def all_to_all(phase, right_ref, table):
        group = LANES // block

        def body(part, carry):
            start = pl.multiple_of(part * LANES, LANES)
            made = dot_first(table[:, pl.ds(start, LANES)], right_ref[...])
            first = part * group
            send_ref[pl.ds(first, group)] = made.astype(BF16).reshape(group, block, width)

            def push(k, inner):
                target = (first + k) * apart

                @pl.when(target != me)
                def _():
                    pltpu.make_async_remote_copy(
                        src_ref=send_ref.at[first + k],
                        dst_ref=recv_ref.at[phase, me],
                        send_sem=send_sem.at[2 * phase],
                        recv_sem=recv_sem.at[2 * phase],
                        device_id=place(target),
                        device_id_type=MESH,
                    ).start()

                return inner

            lax.fori_loop(0, group, push, 0)
            return carry

        lax.fori_loop(0, columns // LANES, body, 0)

    def wait_chunks(ref, count, sem):
        held = ref.shape[0]
        for _ in range(count // held):
            pltpu.make_async_copy(ref, ref, sem).wait()
        if count % held:
            rest = ref.at[pl.ds(0, count % held)]
            pltpu.make_async_copy(rest, rest, sem).wait()

    def wait_owned(ref, sem):
        if_owner(lambda: wait_chunks(ref, owners - 1, sem))
        if apart > 1:
            pl.when(jnp.logical_not(owner))(lambda: wait_chunks(ref, owners, sem))

    def all_to_all_sum(phase):
        recv_ref[phase, me] = send_ref[own]
        wait_chunks(recv_ref.at[phase], n - 1, recv_sem.at[2 * phase])

        def body(k, total):
            return total + recv_ref[phase, k].astype(F32)

        total = lax.fori_loop(0, n, body, jnp.zeros((block, width), F32))

        def lines(part):
            return jnp.concatenate(
                [part[:, k : k + LANES] for k in range(0, width, LANES)], axis=0
            )

        return lines(total[:half]), lines(total[half:])

    parts = width // LANES

    def unlines(part):
        return jnp.concatenate([part[k * half : (k + 1) * half] for k in range(parts)], axis=1)

    def weights(shift):
        real = jnp.concatenate([weight_ref[0, shift]] * parts, axis=0)
        imaginary = jnp.concatenate([weight_ref[1, shift]] * parts, axis=0)
        return real, imaginary

    def all_gather(phase, ref):
        def push(k, carry):
            target = lax.rem(me + k, n)
            pltpu.make_async_remote_copy(
                src_ref=ref.at[own],
                dst_ref=ref.at[own],
                send_sem=send_sem.at[2 * phase + 1],
                recv_sem=recv_sem.at[2 * phase + 1],
                device_id=place(target),
                device_id_type=MESH,
            ).start()
            return carry

        lax.fori_loop(1, n, push, 0)

    def all_gather_wait(phase, ref):
        wait_owned(ref, recv_sem.at[2 * phase + 1])
        if_owner(lambda: wait_chunks(ref, n - 1, send_sem.at[2 * phase + 1]))
        wait_owned(send_ref, send_sem.at[2 * phase])

    all_to_all(0, field_ref, fwd_ref)
    fill(1, inv_ref)

    @if_owner
    def _():
        real, imaginary = all_to_all_sum(0)
        coef_ref[0] = real
        coef_ref[1] = imaginary
        out_real = jnp.zeros_like(real)
        out_imag = jnp.zeros_like(real)
        for shift in range(C):
            w_real, w_imag = weights(shift)
            c_real = group_roll(real, shift)
            c_imag = group_roll(imaginary, shift)
            out_real = out_real + (c_real * w_real - c_imag * w_imag)
            out_imag = out_imag + (c_real * w_imag + c_imag * w_real)
        mixed = jnp.concatenate([unlines(out_real), unlines(out_imag)], axis=0)
        out_ref[own] = mixed.astype(BF16)
        all_gather(0, out_ref)

    all_gather_wait(0, out_ref)

    chunk = 4 * rows_y
    step = mix_ref.shape[0]

    def local(value, matrix):
        return jnp.concatenate(
            [dot(value[:, k : k + step], matrix) for k in range(0, width, step)], axis=1
        )

    def activate(index, carry):
        here = pl.ds(pl.multiple_of(index * chunk, chunk), chunk)
        spectral = dot(inv_ref[here, :], out_ref[...].reshape(columns, width))
        preact = spectral.astype(BF16).astype(F32) + local(field_ref[here, :], mix_ref[...])
        bell = 0.5 * (1.0 + lax.erf(preact * ROOT_HALF))
        tail = preact * jnp.exp(-0.5 * preact * preact) * INV_ROOT_TWO_PI
        slope_ref[here, :] = (bell + tail) * proj_ref[...]
        press_ref[here, :] = split_dot(preact * bell * proj_ref[...], sum_ref[...])
        return carry

    lax.fori_loop(0, cells // chunk, activate, 0)

    def gathered(index):
        made = press_ref[pl.ds(index * per, rows_x, stride=rows_y), :]
        for k in range(1, per):
            other = press_ref[pl.ds(index * per + k, rows_x, stride=rows_y), :]
            made = jnp.where(lane // depth == k, other, made)
        return made

    pressure = jnp.concatenate([gathered(k) for k in range(rows_y // per)], axis=1)
    halo_start(1, pressure)
    halo_wait(0)
    means = [0.5 * (perm + other) for other in neighbours(0, perm)]
    halo_wait(1)

    def operator(turn, value):
        total = jnp.zeros_like(value)
        for mean, other in zip(means, neighbours(turn, value)):
            total = total + mean * (value - other)
        return total

    residual = operator(1, pressure) - forcing_ref[...]
    residual_ref[...] = residual
    halo_start(2, residual)
    halo_wait(2)
    slope_source = operator(2, residual)
    for k in range(rows_y // per):
        piece = slope_source[:, k * LANES : (k + 1) * LANES]
        for j in range(per):
            press_ref[pl.ds(k * per + j, rows_x, stride=rows_y), :] = jnp.where(
                lane // depth == j, piece, 0.0
            )

    def differentiate(index, carry):
        here = pl.ds(pl.multiple_of(index * chunk, chunk), chunk)
        wide = split_dot(press_ref[here, :], spread_ref[...])
        pre_ref[here, :] = (wide * slope_ref[here, :]).astype(BF16)
        return carry

    lax.fori_loop(0, cells // chunk, differentiate, 0)

    all_to_all(1, pre_ref, inv_ref)

    @if_owner
    def _():
        g_real, g_imag = all_to_all_sum(1)
        real = coef_ref[0]
        imaginary = coef_ref[1]
        in_real = jnp.zeros_like(real)
        in_imag = jnp.zeros_like(real)
        grads = [[jnp.zeros((half, LANES), F32) for _ in range(C * C // LANES)] for _ in range(2)]
        spot = lane_iota((half, LANES))
        for shift in range(C):
            w_real, w_imag = weights(shift)
            in_real = in_real + group_roll(g_real * w_real + g_imag * w_imag, (C - shift) % C)
            in_imag = in_imag + group_roll(g_imag * w_real - g_real * w_imag, (C - shift) % C)
            c_real = group_roll(real, shift)
            c_imag = group_roll(imaginary, shift)
            both = (c_real * g_real + c_imag * g_imag, c_real * g_imag - c_imag * g_real)
            for which in range(2):
                total = both[which][:half]
                for k in range(1, parts):
                    total = total + both[which][k * half : (k + 1) * half]
                turn = C
                while turn < LANES:
                    total = total + pltpu.roll(total, turn, 1)
                    turn *= 2
                for k in range(C * C // LANES):
                    source = k * (LANES // C) + spot // C
                    match = (spot % C - source + C) % C == shift
                    grads[which][k] = jnp.where(match, total, grads[which][k])
        message = jnp.concatenate(
            [
                jnp.concatenate([unlines(in_real)] + grads[0], axis=1),
                jnp.concatenate([unlines(in_imag)] + grads[1], axis=1),
            ],
            axis=0,
        )
        gout_ref[own] = message.astype(BF16)
        all_gather(1, gout_ref)

    all_gather_wait(1, gout_ref)

    def finish(index, carry):
        here = pl.ds(pl.multiple_of(index * chunk, chunk), chunk)
        spectral = dot(fwd_ref[here, :], gout_ref[:, :, :width].reshape(columns, width))
        total = spectral.astype(BF16).astype(F32) + local(pre_ref[here, :], mix_t_ref[...])
        grad_ref[here, :] = total.astype(BF16)
        return carry

    lax.fori_loop(0, cells // chunk, finish, 0)

    def report(k, carry):
        terms = gout_ref[k, :, width:].astype(F32)
        spec_ref[0, k] = terms[:half]
        spec_ref[1, k] = terms[half:]
        return carry

    lax.fori_loop(0, owners, report, 0)


def angle_tables(positions, frequencies, length, scale):
    turns = positions[:, None] * frequencies[None, :] % length
    angle = turns.astype(F32) * (2.0 * math.pi / length)
    return (jnp.cos(angle) * scale, jnp.sin(angle) * scale)


def shards(field, perm_class, perm_table, forcing, spec_weight, mix_weight, proj):
    gxn = lax.axis_size("gx")
    gyn = lax.axis_size("gy")
    n = gxn * gyn
    gx = lax.axis_index("gx")
    gy = lax.axis_index("gy")
    me = gx * gyn + gy
    rows_x, rows_y, width = field.shape
    depth = width // C
    cells = rows_x * rows_y
    span_x = rows_x * gxn
    span_y = rows_y * gyn
    owners = min(n, KX * KY // 8)
    modes = KX * KY // owners
    block = 2 * modes
    columns = owners * block

    column = np.arange(columns)
    mode = column // block * modes + column % modes
    imag = jnp.asarray(column % block >= modes)
    f_x = jnp.asarray(mode // KY - KX // 2, jnp.int32)
    f_y = jnp.asarray(mode % KY - KY // 2, jnp.int32)
    at_x = gx * rows_x + jnp.arange(rows_x, dtype=jnp.int32)
    at_y = gy * rows_y + jnp.arange(rows_y, dtype=jnp.int32)
    x_rows, y_rows = [], []
    for x_scale, y_scale in (
        (1.0 / math.sqrt(span_x), 1.0 / math.sqrt(span_y)),
        (1.0 / math.sqrt(KX), 1.0 / math.sqrt(KY)),
    ):
        cosine, sine = angle_tables(at_x, f_x, span_x, x_scale)
        x_cos = cosine.astype(BF16).astype(F32)
        x_sin = (-sine).astype(BF16).astype(F32)
        y_cos, y_sin = angle_tables(at_y, f_y, span_y, y_scale)
        x_rows += [jnp.where(imag, x_sin, x_cos), jnp.where(imag, -x_cos, x_sin)]
        y_rows += [y_cos, y_sin]
    x_rows = jnp.stack(x_rows)
    y_rows = jnp.stack(y_rows)

    own = lax.dynamic_slice_in_dim(spec_weight.reshape(2, KX * KY, C, C), me // (n // owners) * modes, modes, 1)
    own = jnp.tile(own.astype(F32), (1, 1, 1, LANES // C))
    shift = np.arange(C)[:, None, None]
    source = np.arange(C)[None, :, None]
    output = np.arange(LANES)[None, None, :] % C
    chosen = jnp.asarray((output - shift) % C == source)
    skewed = jnp.sum(jnp.where(chosen[None, :, None], own[:, None], 0.0), axis=3)

    step = min(256, width)
    copies = step // C
    eye = jnp.asarray(np.kron(np.eye(copies), np.ones((C, C))), BF16)
    mix = jnp.tile(mix_weight, (copies, copies)) * eye
    mix_t = jnp.tile(mix_weight.T, (copies, copies)) * eye
    proj_row = jnp.tile(proj, depth).reshape(1, width)
    gather = np.arange(width)[:, None] // C == np.arange(LANES)[None, :] % depth
    total = jnp.asarray(gather, BF16)
    spread = jnp.asarray(gather.T, BF16)

    vmem = pl.BlockSpec(memory_space=pltpu.VMEM)
    smem = pl.BlockSpec(memory_space=pltpu.SMEM)
    residual, grad_field, spec = pl.pallas_call(
        functools.partial(kernel, gxn, gyn, owners, rows_x, rows_y, depth),
        out_shape=(
            jax.ShapeDtypeStruct((rows_x, rows_y * depth), F32),
            jax.ShapeDtypeStruct((cells, width), BF16),
            jax.ShapeDtypeStruct((2, owners, modes, C * C), F32),
        ),
        in_specs=[vmem, vmem, smem] + [vmem] * 9,
        out_specs=(vmem, vmem, vmem),
        scratch_shapes=[
            pltpu.VMEM((cells, columns), BF16),
            pltpu.VMEM((cells, columns), BF16),
            pltpu.VMEM((owners, block, width), BF16),
            pltpu.VMEM((2, n, block, width), BF16),
            pltpu.VMEM((owners, block, width), BF16),
            pltpu.VMEM((owners, block, width + C * C), BF16),
            pltpu.VMEM((cells, width), F32),
            pltpu.VMEM((cells, width), BF16),
            pltpu.VMEM((cells, LANES), F32),
            pltpu.VMEM((2, modes * width // LANES, LANES), F32),
            pltpu.VMEM((3, 2, 1, rows_y * depth), F32),
            pltpu.VMEM((3, 2, 1, rows_y * depth), F32),
            pltpu.VMEM((3, 2, rows_x, LANES), F32),
            pltpu.VMEM((3, 2, rows_x, LANES), F32),
            pltpu.SemaphoreType.DMA((4,)),
            pltpu.SemaphoreType.DMA((4,)),
            pltpu.SemaphoreType.DMA((3, 4)),
            pltpu.SemaphoreType.DMA((3, 4)),
        ],
        compiler_params=pltpu.CompilerParams(
            collective_id=0, has_side_effects=True, vmem_limit_bytes=60 * 1024 * 1024
        ),
        name="fourier_darcy",
    )(
        field.reshape(cells, width),
        perm_class,
        perm_table,
        forcing,
        x_rows,
        y_rows,
        skewed,
        mix,
        mix_t,
        proj_row,
        total,
        spread,
    )
    spec_grad = spec.reshape(2, KX, KY, C, C)
    return (residual, grad_field.reshape(rows_x, rows_y, width), spec_grad)


def solution(mesh):
    placed = (P("gx", "gy", None), P("gx", "gy"), P(), P("gx", "gy"), P(), P(), P())
    return jax.shard_map(
        shards,
        mesh=mesh,
        in_specs=placed,
        out_specs=(P("gx", "gy"), P("gx", "gy", None), P()),
        check_vma=False,
    )
```

time: 667 us -> 110 us (0.16)
  the two profiles are of different devices: /device:TPU:0 before, /device:TPU:27 now
where the time goes in v1:
time: 110 us
  Pallas kernels  91.2 us (83%)
  local copies, waits for them, and re-layouts  11.7 us (11%)
  other arithmetic  6.11 us (6%)
    pallas_call x1, Pallas kernels, shards(): pl.pallas_call(functools.partial(kernel, gxn, gyn, owners, rows_x, rows_y...  91.2 us
    reshape x1, local copies, waits for them, and re-layouts, shards(): spec_grad = spec.reshape(2, KX, KY, C, C)  3.84 us

profile of v1, /device:TPU:27, one launch (start us, length us, event | category | flops | bytes accessed | tf_op | source)
XLA Modules:
  0.0 109.7 jit_solution(10807605478754818530)
XLA Ops:
  0.7 0.8 copy.19
  1.4 0.7 tile.38
  2.1 0.7 reshape_tile.3.proj_ref
  2.8 0.8 dynamic-slice_convert_fusion
  3.6 1.0 convert_select_fusion.2
  4.7 0.7 pad_maximum_fusion.1.x_ref
  5.4 0.0 copy-start.3
  5.4 0.0 copy-start.1
  5.4 0.0 copy-start.4
  5.4 1.4 %broadcast_multiply_fusion.5 = (f32[1,64,512]{2,1,0:T(8,128)S(1)}, f32[1,64,512]{2,1,0:T(8,128)S(1)}, f32[1,64,512]{2,1,0:T(8,128)S(1)}, f32[1,64,512]{2,1,0:T(8,128)S(1)}) fusion(s32[512]{0:T(512)} %constant.94.clone, s32[64]{0:T(128)S(1)} %iota_add_fusion), kind=kLoop, calls=%fused_computation.31 | loop fusion | flops 589824 | bytes 526592 | tf_op jit(solution)/shard_map/mul | solution.py:446
  6.8 0.8 pad_maximum_fusion.y_ref
  7.6 0.1 tile.14
  7.7 0.3 tile.15
  8.0 0.0 copy-done.3
  8.0 1.1 %select_reduce_fusion.weight_ref = f32[2,16,8,128]{3,2,1,0:T(8,128)} fusion(f32[2,8,16,128]{3,2,1,0:T(8,128)S(1)} %tile.15, pred[16,16,128]{2,1,0:T(8,128)(4,1)S(1)} %copy-done.3), kind=kLoop, calls=%fused_computation | loop fusion | flops 1015808 | bytes 294912 | tf_op jit(solution)/shard_map/reduce_sum | solution.py:493
  9.2 0.0 copy-done.1
  9.2 0.0 copy-done.4
  9.2 0.1 broadcast_multiply_fusion
  9.3 1.7 %reshape.607.mix_t_ref = bf16[256,256]{1,0:T(8,128)(2,1)} reshape(bf16[16,16,16,16]{3,2,1,0:T(8,128)(2,1)S(1)} %get-tuple-element.9) | data formatting | bytes 262144 | tf_op jit(solution)/shard_map/mul | solution.py:499
  11.0 1.6 %reshape.605.mix_ref = bf16[256,256]{1,0:T(8,128)(2,1)} reshape(bf16[16,16,16,16]{3,2,1,0:T(8,128)(2,1)S(1)} %get-tuple-element.10) | data formatting | bytes 262144 | tf_op jit(solution)/shard_map/mul | solution.py:498
  12.6 91.2 %fourier_darcy.1 = (f32[32,2048]{1,0:T(8,128)}, bf16[2048,512]{1,0:T(8,128)(2,1)}, f32[2,32,8,256]{3,2,1,0:T(8,128)}) custom-call(bf16[2048,512]{1,0:T(8,128)(2,1)} %bitcast.13, s32[32,2048]{1,0:T(8,128)} %class_ref.1, f32[8]{0:T(128)} %table_ref.1, f32[32,2048]{1,0:T(8,128)} %forcing_ref.1, f32[4,32,512]{2,1,0:T(8,128)} %pad_maximum_fusion.1.x_ref, ...), custom_call_target="tpu_custom_call" | custom-call | tf_op jit(solution)/shard_map/fourier_darcy/pallas_call | solution.py:507
  103.8 0.0 copy-start.2
  103.8 0.0 copy-start
  103.8 3.8 %reshape.603 = f32[2,16,16,16,16]{4,3,2,1,0:T(8,128)} reshape(f32[2,32,8,256]{3,2,1,0:T(8,128)} %get-tuple-element.8) | data formatting | bytes 1048576 | tf_op jit(solution)/shard_map/reshape | solution.py:554
  107.7 0.0 copy-done.2
  107.7 0.7 copy.22
  108.4 0.0 copy-done
  108.4 1.3 %copy.23 = bf16[32,64,512]{2,1,0:T(8,128)(2,1)} copy(bf16[32,64,512]{2,1,0:T(8,128)(2,1)S(1)} %bitcast.12) | data formatting | bytes 4194304
  (2 shorter events, 0.0 us)
Async XLA Ops:
  5.4 2.6 %copy-start.3 = (pred[16,16,128]{2,1,0:T(8,128)(4,1)S(1)}, pred[16,16,128]{2,1,0:T(8,128)(4,1)}, u32[]{:S(2)}) copy-start(pred[16,16,128]{2,1,0:T(8,128)(4,1)} %constant.95.clone) | copy-start | bytes 98308
  5.4 3.8 %copy-start.1 = (bf16[16,16,16,16]{3,2,1,0:T(8,128)(2,1)S(1)}, bf16[16,16,16,16]{3,2,1,0:T(8,128)(2,1)}, u32[]{:S(2)}) copy-start(bf16[16,16,16,16]{3,2,1,0:T(8,128)(2,1)} %constant.99) | copy-start | bytes 393220
  5.4 3.8 %copy-start.4 = (bf16[16,16]{1,0:T(8,128)(2,1)S(1)}, bf16[16,16]{1,0:T(8,128)(2,1)}, u32[]{:S(2)}) copy-start(bf16[16,16]{1,0:T(8,128)(2,1)} %param.19) | copy-start | bytes 1540
  103.8 3.9 %copy-start.2 = (f32[32,2048]{1,0:T(8,128)S(1)}, f32[32,2048]{1,0:T(8,128)}, u32[]{:S(2)}) copy-start(f32[32,2048]{1,0:T(8,128)} %get-tuple-element.22) | copy-start | bytes 786436
  103.8 4.6 %copy-start = (bf16[2048,512]{1,0:T(8,128)(2,1)S(1)}, bf16[2048,512]{1,0:T(8,128)(2,1)}, u32[]{:S(2)}) copy-start(bf16[2048,512]{1,0:T(8,128)(2,1)} %get-tuple-element.7) | copy-start | bytes 6291460

commit v2 on v1

--- a/solution.py
+++ b/solution.py
@@ -62,11 +62,8 @@
     x_ref,
     y_ref,
     weight_ref,
-    mix_ref,
-    mix_t_ref,
-    proj_ref,
-    sum_ref,
-    spread_ref,
+    mixing_ref,
+    proj_in,
     residual_ref,
     grad_ref,
     spec_ref,
@@ -80,6 +77,14 @@
     pre_ref,
     press_ref,
     coef_ref,
+    pair_ref,
+    half_ref,
+    skew_ref,
+    mix_ref,
+    mix_t_ref,
+    proj_ref,
+    sum_ref,
+    spread_ref,
     x_send,
     x_recv,
     y_send,
@@ -92,10 +97,13 @@
     n = gxn * gyn
     gx = lax.axis_index("gx")
     gy = lax.axis_index("gy")
-    me = gx * gyn + gy
+    core = gx % 2
+    chips = n // 2
+    chip = gx // 2 * gyn + gy
     apart = n // owners
-    own = me // apart
-    owner = me % apart == 0
+    group = owners // 2
+    own = core * group + chip // apart
+    owner = chip % apart == 0
     cells = rows_x * rows_y
     width = depth * C
     block = 2 * KX * KY // owners
@@ -111,30 +119,60 @@
             pl.when(owner)(body)
 
     def place(index):
-        return (index // gyn, index % gyn)
-
+        return (2 * (index // gyn) + core, index % gyn)
+
+    sibling = (gx + 1 - 2 * core, gy)
+    beside = gx - 1 + 2 * core
+    has_beside = jnp.logical_and(beside >= 0, beside < gxn)
     barrier = pltpu.get_barrier_semaphore()
 
     def greet(k, carry):
-        target = lax.rem(me + k, n)
+        target = lax.rem(chip + k, chips)
         pl.semaphore_signal(barrier, inc=1, device_id=place(target), device_id_type=MESH)
         return carry
 
-    lax.fori_loop(1, n, greet, 0)
+    lax.fori_loop(1, chips, greet, 0)
+    pl.semaphore_signal(barrier, inc=1, device_id=sibling, device_id_type=MESH)
+
+    @pl.when(has_beside)
+    def _():
+        pl.semaphore_signal(barrier, inc=1, device_id=(beside, gy), device_id_type=MESH)
+
+    def chosen(shape, rule):
+        row_at = lax.broadcasted_iota(jnp.int32, shape, 0)
+        lane_at = lax.broadcasted_iota(jnp.int32, shape, 1)
+        return rule(row_at, lane_at)
+
+    def ones(shape, rule):
+        return jnp.where(chosen(shape, rule), 1.0, 0.0).astype(BF16)
+
+    def tables(which):
+        shape = (LANES, columns)
+        slot = lax.broadcasted_iota(jnp.int32, shape, 0)
+        column = lax.broadcasted_iota(jnp.int32, shape, 1)
+        mode = column // block * half + column % half
+        first_mode = mode // KY + 2 * KX * which
+        second_mode = mode % KY + 2 * KY * which
+        imaginary = column % block >= half
+        x_here = x_ref[pl.ds(pl.multiple_of(gx * rows_x, rows_x), rows_x), :]
+        y_here = y_ref[pl.ds(pl.multiple_of(gy * rows_y, rows_y), rows_y), :]
+        cosine = jnp.where(slot == first_mode, 1.0, 0.0)
+        sine = jnp.where(slot == first_mode + KX, 1.0, 0.0)
+        first = dot(x_here, jnp.where(imaginary, sine, cosine).astype(BF16))
+        second = dot(x_here, jnp.where(imaginary, -cosine, sine).astype(BF16))
+        fine = slot % (LANES // 2)
+        y_cos = dot(y_here, jnp.where(fine == second_mode, 1.0, 0.0).astype(BF16))
+        y_sin = dot(y_here, jnp.where(fine == second_mode + KY, 1.0, 0.0).astype(BF16))
+        return first, second, y_cos, y_sin
 
     def fill(which, ref):
-        def body(x, carry):
-            first = x_ref[2 * which, pl.ds(x, 1), :]
-            second = x_ref[2 * which + 1, pl.ds(x, 1), :]
-            made = first * y_ref[2 * which] + second * y_ref[2 * which + 1]
-            start = pl.multiple_of(x * rows_y, rows_y)
-            ref[pl.ds(start, rows_y), :] = made.astype(BF16)
-            return carry
-
-        lax.fori_loop(0, rows_x, body, 0)
+        first, second, y_cos, y_sin = tables(which)
+        for x in range(rows_x):
+            made = first[x : x + 1] * y_cos + second[x : x + 1] * y_sin
+            ref[x * rows_y : (x + 1) * rows_y, :] = made.astype(BF16)
 
     fill(0, fwd_ref)
-    pl.semaphore_wait(barrier, n - 1)
+    pl.semaphore_wait(barrier, chips + jnp.where(has_beside, 1, 0))
 
     classes = class_ref[...]
     perm = jnp.zeros(classes.shape, F32)
@@ -210,35 +248,15 @@
 
     halo_start(0, perm)
 
-    def all_to_all(phase, right_ref, table):
-        group = LANES // block
-
-        def body(part, carry):
-            start = pl.multiple_of(part * LANES, LANES)
-            made = dot_first(table[:, pl.ds(start, LANES)], right_ref[...])
-            first = part * group
-            send_ref[pl.ds(first, group)] = made.astype(BF16).reshape(group, block, width)
-
-            def push(k, inner):
-                target = (first + k) * apart
-
-                @pl.when(target != me)
-                def _():
-                    pltpu.make_async_remote_copy(
-                        src_ref=send_ref.at[first + k],
-                        dst_ref=recv_ref.at[phase, me],
-                        send_sem=send_sem.at[2 * phase],
-                        recv_sem=recv_sem.at[2 * phase],
-                        device_id=place(target),
-                        device_id_type=MESH,
-                    ).start()
-
-                return inner
-
-            lax.fori_loop(0, group, push, 0)
-            return carry
-
-        lax.fori_loop(0, columns // LANES, body, 0)
+    def to_sibling(source, landing, sem):
+        return pltpu.make_async_remote_copy(
+            src_ref=source,
+            dst_ref=landing,
+            send_sem=send_sem.at[sem],
+            recv_sem=recv_sem.at[sem],
+            device_id=sibling,
+            device_id_type=MESH,
+        )
 
     def wait_chunks(ref, count, sem):
         held = ref.shape[0]
@@ -249,18 +267,55 @@
             pltpu.make_async_copy(rest, rest, sem).wait()
 
     def wait_owned(ref, sem):
-        if_owner(lambda: wait_chunks(ref, owners - 1, sem))
+        some = ref.at[pl.ds(0, group)]
+        if_owner(lambda: wait_chunks(some, group - 1, sem))
         if apart > 1:
-            pl.when(jnp.logical_not(owner))(lambda: wait_chunks(ref, owners, sem))
+            pl.when(jnp.logical_not(owner))(lambda: wait_chunks(some, group, sem))
+
+    mine = pl.ds(core * group, group)
+    theirs = pl.ds((1 - core) * group, group)
+
+    def all_to_all(phase, right_ref, table):
+        lanes = group * block
+
+        def product(which):
+            start = pl.multiple_of(which * lanes, lanes)
+            return dot_first(table[:, pl.ds(start, lanes)], right_ref[...])
+
+        send_ref[theirs] = product(1 - core).astype(BF16).reshape(group, block, width)
+        pair = to_sibling(send_ref.at[theirs], pair_ref.at[phase], 4 * phase)
+        pair.start()
+        half_ref[...] = product(core)
+        pair.wait()
+        total = half_ref[...] + pair_ref[phase].reshape(lanes, width).astype(F32)
+        send_ref[mine] = total.astype(BF16).reshape(group, block, width)
+
+        def push(k, carry):
+            target = k * apart
+
+            @pl.when(target != chip)
+            def _():
+                pltpu.make_async_remote_copy(
+                    src_ref=send_ref.at[core * group + k],
+                    dst_ref=recv_ref.at[phase, chip],
+                    send_sem=send_sem.at[4 * phase + 1],
+                    recv_sem=recv_sem.at[4 * phase + 1],
+                    device_id=place(target),
+                    device_id_type=MESH,
+                ).start()
+
+            return carry
+
+        lax.fori_loop(0, group, push, 0)
 
     def all_to_all_sum(phase):
-        recv_ref[phase, me] = send_ref[own]
-        wait_chunks(recv_ref.at[phase], n - 1, recv_sem.at[2 * phase])
+        recv_ref[phase, chip] = send_ref[own]
+        wait_chunks(recv_ref.at[phase], chips - 1, recv_sem.at[4 * phase + 1])
 
         def body(k, total):
             return total + recv_ref[phase, k].astype(F32)
 
-        total = lax.fori_loop(0, n, body, jnp.zeros((block, width), F32))
+        total = lax.fori_loop(0, chips, body, jnp.zeros((block, width), F32))
 
         def lines(part):
             return jnp.concatenate(
@@ -275,32 +330,60 @@
         return jnp.concatenate([part[k * half : (k + 1) * half] for k in range(parts)], axis=1)
 
     def weights(shift):
-        real = jnp.concatenate([weight_ref[0, shift]] * parts, axis=0)
-        imaginary = jnp.concatenate([weight_ref[1, shift]] * parts, axis=0)
+        real = jnp.concatenate([skew_ref[shift, :half]] * parts, axis=0)
+        imaginary = jnp.concatenate([skew_ref[shift, half:]] * parts, axis=0)
         return real, imaginary
 
     def all_gather(phase, ref):
         def push(k, carry):
-            target = lax.rem(me + k, n)
+            target = lax.rem(chip + k, chips)
             pltpu.make_async_remote_copy(
                 src_ref=ref.at[own],
                 dst_ref=ref.at[own],
-                send_sem=send_sem.at[2 * phase + 1],
-                recv_sem=recv_sem.at[2 * phase + 1],
+                send_sem=send_sem.at[4 * phase + 2],
+                recv_sem=recv_sem.at[4 * phase + 2],
                 device_id=place(target),
                 device_id_type=MESH,
             ).start()
             return carry
 
-        lax.fori_loop(1, n, push, 0)
+        lax.fori_loop(1, chips, push, 0)
 
     def all_gather_wait(phase, ref):
-        wait_owned(ref, recv_sem.at[2 * phase + 1])
-        if_owner(lambda: wait_chunks(ref, n - 1, send_sem.at[2 * phase + 1]))
-        wait_owned(send_ref, send_sem.at[2 * phase])
+        wait_owned(ref, recv_sem.at[4 * phase + 2])
+        pair = to_sibling(ref.at[mine], ref.at[mine], 4 * phase + 3)
+        pair.start()
+        pair.wait()
+        if_owner(
+            lambda: wait_chunks(ref.at[pl.ds(0, group)], chips - 1, send_sem.at[4 * phase + 2])
+        )
+        wait_owned(send_ref, send_sem.at[4 * phase + 1])
 
     all_to_all(0, field_ref, fwd_ref)
     fill(1, inv_ref)
+    step = mix_ref.shape[0]
+    repeat = ones((step, C), lambda r, l: r % C == l)
+    repeat_t = ones((C, step), lambda r, l: r == l % C)
+    blocks = chosen((step, step), lambda r, l: r // C == l // C)
+    tall = dot(repeat, mixing_ref[...]).astype(BF16)
+    mix_ref[...] = jnp.where(blocks, dot(tall, repeat_t), 0.0).astype(BF16)
+    tall = lax.dot_general(
+        repeat, mixing_ref[...], (((1,), (1,)), ((), ())), preferred_element_type=F32
+    ).astype(BF16)
+    mix_t_ref[...] = jnp.where(blocks, dot(tall, repeat_t), 0.0).astype(BF16)
+    sum_ref[...] = ones(sum_ref.shape, lambda r, l: r // C == l % depth)
+    spread_ref[...] = ones(spread_ref.shape, lambda r, l: l // C == r % depth)
+    channel = lane_iota((1, width)) % C
+    proj_row = jnp.zeros((1, width), F32)
+    for k in range(C):
+        proj_row = jnp.where(channel == k, proj_in[k], proj_row)
+    proj_ref[...] = proj_row
+    for shift in range(C):
+        pick = ones(
+            (C * C, LANES),
+            lambda r, l: (r % C == l % C) & (r // C == (l % C - shift + C) % C),
+        )
+        skew_ref[shift] = dot(weight_ref[...], pick)
 
     @if_owner
     def _():
@@ -322,7 +405,6 @@
     all_gather_wait(0, out_ref)
 
     chunk = 4 * rows_y
-    step = mix_ref.shape[0]
 
     def local(value, matrix):
         return jnp.concatenate(
@@ -440,10 +522,30 @@
     lax.fori_loop(0, owners, report, 0)
 
 
-def angle_tables(positions, frequencies, length, scale):
-    turns = positions[:, None] * frequencies[None, :] % length
-    angle = turns.astype(F32) * (2.0 * math.pi / length)
-    return (jnp.cos(angle) * scale, jnp.sin(angle) * scale)
+def angle_tables(length, count, scale):
+    frequencies = np.arange(count) - count // 2
+    turns = np.arange(length)[:, None] * frequencies[None, :] % length
+    angle = turns.astype(np.float32) * np.float32(2.0 * math.pi / length)
+    return np.cos(angle) * np.float32(scale), np.sin(angle) * np.float32(scale)
+
+
+def x_table(length):
+    parts = []
+    for scale in (1.0 / math.sqrt(length), 1.0 / math.sqrt(KX)):
+        cosine, sine = angle_tables(length, KX, scale)
+        parts += [cosine, -sine]
+    table = np.concatenate(parts, axis=1)
+    return np.pad(table, ((0, 0), (0, LANES - table.shape[1]))).astype(BF16)
+
+
+def y_table(length):
+    parts = []
+    for scale in (1.0 / math.sqrt(length), 1.0 / math.sqrt(KY)):
+        parts += list(angle_tables(length, KY, scale))
+    table = np.concatenate(parts, axis=1)
+    high = table.astype(BF16)
+    low = (table - high.astype(np.float32)).astype(BF16)
+    return np.concatenate([high, low], axis=1)
 
 
 def shards(field, perm_class, perm_table, forcing, spec_weight, mix_weight, proj):
@@ -452,7 +554,6 @@
     n = gxn * gyn
     gx = lax.axis_index("gx")
     gy = lax.axis_index("gy")
-    me = gx * gyn + gy
     rows_x, rows_y, width = field.shape
     depth = width // C
     cells = rows_x * rows_y
@@ -462,45 +563,11 @@
     modes = KX * KY // owners
     block = 2 * modes
     columns = owners * block
-
-    column = np.arange(columns)
-    mode = column // block * modes + column % modes
-    imag = jnp.asarray(column % block >= modes)
-    f_x = jnp.asarray(mode // KY - KX // 2, jnp.int32)
-    f_y = jnp.asarray(mode % KY - KY // 2, jnp.int32)
-    at_x = gx * rows_x + jnp.arange(rows_x, dtype=jnp.int32)
-    at_y = gy * rows_y + jnp.arange(rows_y, dtype=jnp.int32)
-    x_rows, y_rows = [], []
-    for x_scale, y_scale in (
-        (1.0 / math.sqrt(span_x), 1.0 / math.sqrt(span_y)),
-        (1.0 / math.sqrt(KX), 1.0 / math.sqrt(KY)),
-    ):
-        cosine, sine = angle_tables(at_x, f_x, span_x, x_scale)
-        x_cos = cosine.astype(BF16).astype(F32)
-        x_sin = (-sine).astype(BF16).astype(F32)
-        y_cos, y_sin = angle_tables(at_y, f_y, span_y, y_scale)
-        x_rows += [jnp.where(imag, x_sin, x_cos), jnp.where(imag, -x_cos, x_sin)]
-        y_rows += [y_cos, y_sin]
-    x_rows = jnp.stack(x_rows)
-    y_rows = jnp.stack(y_rows)
-
-    own = lax.dynamic_slice_in_dim(spec_weight.reshape(2, KX * KY, C, C), me // (n // owners) * modes, modes, 1)
-    own = jnp.tile(own.astype(F32), (1, 1, 1, LANES // C))
-    shift = np.arange(C)[:, None, None]
-    source = np.arange(C)[None, :, None]
-    output = np.arange(LANES)[None, None, :] % C
-    chosen = jnp.asarray((output - shift) % C == source)
-    skewed = jnp.sum(jnp.where(chosen[None, :, None], own[:, None], 0.0), axis=3)
-
+    own = gx % 2 * (owners // 2) + (gx // 2 * gyn + gy) // (n // owners)
+    weights = lax.dynamic_slice_in_dim(
+        spec_weight.reshape(2, KX * KY, C, C), own * modes, modes, 1
+    ).reshape(block, C * C)
     step = min(256, width)
-    copies = step // C
-    eye = jnp.asarray(np.kron(np.eye(copies), np.ones((C, C))), BF16)
-    mix = jnp.tile(mix_weight, (copies, copies)) * eye
-    mix_t = jnp.tile(mix_weight.T, (copies, copies)) * eye
-    proj_row = jnp.tile(proj, depth).reshape(1, width)
-    gather = np.arange(width)[:, None] // C == np.arange(LANES)[None, :] % depth
-    total = jnp.asarray(gather, BF16)
-    spread = jnp.asarray(gather.T, BF16)
 
     vmem = pl.BlockSpec(memory_space=pltpu.VMEM)
     smem = pl.BlockSpec(memory_space=pltpu.SMEM)
@@ -511,25 +578,33 @@
             jax.ShapeDtypeStruct((cells, width), BF16),
             jax.ShapeDtypeStruct((2, owners, modes, C * C), F32),
         ),
-        in_specs=[vmem, vmem, smem] + [vmem] * 9,
+        in_specs=[vmem, vmem, smem] + [vmem] * 5 + [smem],
         out_specs=(vmem, vmem, vmem),
         scratch_shapes=[
             pltpu.VMEM((cells, columns), BF16),
             pltpu.VMEM((cells, columns), BF16),
             pltpu.VMEM((owners, block, width), BF16),
-            pltpu.VMEM((2, n, block, width), BF16),
+            pltpu.VMEM((2, n // 2, block, width), BF16),
             pltpu.VMEM((owners, block, width), BF16),
             pltpu.VMEM((owners, block, width + C * C), BF16),
             pltpu.VMEM((cells, width), F32),
             pltpu.VMEM((cells, width), BF16),
             pltpu.VMEM((cells, LANES), F32),
             pltpu.VMEM((2, modes * width // LANES, LANES), F32),
+            pltpu.VMEM((2, owners // 2, block, width), BF16),
+            pltpu.VMEM((columns // 2, width), F32),
+            pltpu.VMEM((C, block, LANES), F32),
+            pltpu.VMEM((step, step), BF16),
+            pltpu.VMEM((step, step), BF16),
+            pltpu.VMEM((1, width), F32),
+            pltpu.VMEM((width, LANES), BF16),
+            pltpu.VMEM((LANES, width), BF16),
             pltpu.VMEM((3, 2, 1, rows_y * depth), F32),
             pltpu.VMEM((3, 2, 1, rows_y * depth), F32),
             pltpu.VMEM((3, 2, rows_x, LANES), F32),
             pltpu.VMEM((3, 2, rows_x, LANES), F32),
-            pltpu.SemaphoreType.DMA((4,)),
-            pltpu.SemaphoreType.DMA((4,)),
+            pltpu.SemaphoreType.DMA((8,)),
+            pltpu.SemaphoreType.DMA((8,)),
             pltpu.SemaphoreType.DMA((3, 4)),
             pltpu.SemaphoreType.DMA((3, 4)),
         ],
@@ -542,14 +617,11 @@
         perm_class,
         perm_table,
         forcing,
-        x_rows,
-        y_rows,
-        skewed,
-        mix,
-        mix_t,
-        proj_row,
-        total,
-        spread,
+        jnp.asarray(x_table(span_x)),
+        jnp.asarray(y_table(span_y)),
+        weights,
+        mix_weight,
+        proj,
     )
     spec_grad = spec.reshape(2, KX, KY, C, C)
     return (residual, grad_field.reshape(rows_x, rows_y, width), spec_grad)

time: 110 us -> 83.3 us (0.76)
  the two profiles are of different devices: /device:TPU:27 before, /device:TPU:0 now
where the time goes in v2:
time: 83.3 us; the launch traced here: 82.7 us
  Pallas kernels  72.2 us (87%)
  local copies, waits for them, and re-layouts  9.85 us (12%)
    pallas_call x1, Pallas kernels, shards(): pl.pallas_call(functools.partial(kernel, gxn, gyn, owners, rows_x, rows_y...  72.2 us
    unnamed x6, local copies, waits for them, and re-layouts  5.4 us
    reshape x1, local copies, waits for them, and re-layouts, shards(): spec_grad = spec.reshape(2, KX, KY, C, C)  3.73 us

profile of v2, /device:TPU:0, one launch (start us, length us, event | category | flops | bytes accessed | tf_op | source)
XLA Modules:
  0.0 82.7 jit_solution(14115113610899467286)
XLA Ops:
  0.6 0.0 copy-start
  0.7 1.6 %copy-done = bf16[2,16,16,16,16]{4,3,2,1,0:T(8,128)(2,1)S(1)} copy-done((bf16[2,16,16,16,16]{4,3,2,1,0:T(8,128)(2,1)S(1)}, bf16[2,16,16,16,16]{4,3,2,1,0:T(8,128)(2,1)}, u32[]{:S(2)}) %copy-start) | copy-done | bytes 262168
  2.2 0.7 reshape.23.weight_ref
  3.0 72.2 %fourier_darcy.1 = (f32[32,2048]{1,0:T(8,128)}, bf16[2048,512]{1,0:T(8,128)(2,1)}, f32[2,32,8,256]{3,2,1,0:T(8,128)}) custom-call(bf16[2048,512]{1,0:T(8,128)(2,1)} %bitcast.8, s32[32,2048]{1,0:T(8,128)} %class_ref.1, f32[8]{0:T(128)} %table_ref.1, f32[32,2048]{1,0:T(8,128)} %forcing_ref.1, bf16[512,128]{1,0:T(8,128)(2,1)} %constant.52.clone.x_ref, ...), custom_call_target="tpu_custom_call" | custom-call | tf_op jit(solution)/shard_map/fourier_darcy/pallas_call | solution.py:574
  75.1 0.0 copy-start.1
  75.1 3.7 %reshape.25 = f32[2,16,16,16,16]{4,3,2,1,0:T(8,128)} reshape(f32[2,32,8,256]{3,2,1,0:T(8,128)} %get-tuple-element.8) | data formatting | bytes 1048576 | tf_op jit(solution)/shard_map/reshape | solution.py:626
  78.9 0.0 copy-done.1
  78.9 0.7 copy.14
  79.6 3.1 %copy.15 = bf16[32,64,512]{2,1,0:T(8,128)(2,1)} copy(bf16[32,64,512]{2,1,0:T(8,128)(2,1)} %bitcast.9) | data formatting | bytes 4194304
  (1 shorter events, 0.0 us)
Async XLA Ops:
  0.6 1.6 %copy-start = (bf16[2,16,16,16,16]{4,3,2,1,0:T(8,128)(2,1)S(1)}, bf16[2,16,16,16,16]{4,3,2,1,0:T(8,128)(2,1)}, u32[]{:S(2)}) copy-start(bf16[2,16,16,16,16]{4,3,2,1,0:T(8,128)(2,1)} %param.13) | copy-start | bytes 786436
  75.1 3.7 %copy-start.1 = (f32[32,2048]{1,0:T(8,128)S(1)}, f32[32,2048]{1,0:T(8,128)}, u32[]{:S(2)}) copy-start(f32[32,2048]{1,0:T(8,128)} %get-tuple-element.12) | copy-start | bytes 786436

commit v3 on v2

--- a/solution.py
+++ b/solution.py
@@ -14,6 +14,7 @@
 KY = 16
 CLASSES = 8
 LANES = 128
+HALVES = 2
 ROOT_HALF = 0.7071067811865476
 INV_ROOT_TWO_PI = 0.3989422804014327
 MESH = pl.DeviceIdType.MESH
@@ -73,6 +74,8 @@
     recv_ref,
     out_ref,
     gout_ref,
+    terms_ref,
+    total_ref,
     slope_ref,
     pre_ref,
     press_ref,
@@ -110,6 +113,8 @@
     half = block // 2
     per = LANES // depth
     span = rows_y * depth
+    wide = width // HALVES
+    parts = wide // LANES
     columns = owners * block
 
     def if_owner(body):
@@ -275,20 +280,35 @@
     mine = pl.ds(core * group, group)
     theirs = pl.ds((1 - core) * group, group)
 
-    def all_to_all(phase, right_ref, table):
-        lanes = group * block
-
-        def product(which):
-            start = pl.multiple_of(which * lanes, lanes)
-            return dot_first(table[:, pl.ds(start, lanes)], right_ref[...])
-
-        send_ref[theirs] = product(1 - core).astype(BF16).reshape(group, block, width)
-        pair = to_sibling(send_ref.at[theirs], pair_ref.at[phase], 4 * phase)
-        pair.start()
-        half_ref[...] = product(core)
-        pair.wait()
-        total = half_ref[...] + pair_ref[phase].reshape(lanes, width).astype(F32)
-        send_ref[mine] = total.astype(BF16).reshape(group, block, width)
+    lanes = group * block
+
+    def sem(phase, piece, stage):
+        return (phase * HALVES + piece) * 4 + stage
+
+    def strip(piece):
+        return slice(piece * wide, (piece + 1) * wide)
+
+    def product(which, piece, right_ref, table):
+        start = pl.multiple_of(which * lanes, lanes)
+        return dot_first(table[:, pl.ds(start, lanes)], right_ref[:, strip(piece)])
+
+    def pair_copy(phase, piece):
+        return to_sibling(
+            send_ref.at[piece, theirs], pair_ref.at[phase, piece], sem(phase, piece, 0)
+        )
+
+    def give(phase, piece, right_ref, table):
+        made = product(1 - core, piece, right_ref, table)
+        send_ref[piece, theirs] = made.astype(BF16).reshape(group, block, wide)
+        pair_copy(phase, piece).start()
+
+    def keep(piece, right_ref, table):
+        half_ref[piece] = product(core, piece, right_ref, table)
+
+    def send(phase, piece):
+        pair_copy(phase, piece).wait()
+        total = half_ref[piece] + pair_ref[phase, piece].reshape(lanes, wide).astype(F32)
+        send_ref[piece, mine] = total.astype(BF16).reshape(group, block, wide)
 
         def push(k, carry):
             target = k * apart
@@ -296,10 +316,10 @@
             @pl.when(target != chip)
             def _():
                 pltpu.make_async_remote_copy(
-                    src_ref=send_ref.at[core * group + k],
-                    dst_ref=recv_ref.at[phase, chip],
-                    send_sem=send_sem.at[4 * phase + 1],
-                    recv_sem=recv_sem.at[4 * phase + 1],
+                    src_ref=send_ref.at[piece, core * group + k],
+                    dst_ref=recv_ref.at[phase, piece, chip],
+                    send_sem=send_sem.at[sem(phase, piece, 1)],
+                    recv_sem=recv_sem.at[sem(phase, piece, 1)],
                     device_id=place(target),
                     device_id_type=MESH,
                 ).start()
@@ -308,23 +328,19 @@
 
         lax.fori_loop(0, group, push, 0)
 
-    def all_to_all_sum(phase):
-        recv_ref[phase, chip] = send_ref[own]
-        wait_chunks(recv_ref.at[phase], chips - 1, recv_sem.at[4 * phase + 1])
+    def collect(phase, piece):
+        recv_ref[phase, piece, chip] = send_ref[piece, own]
+        wait_chunks(recv_ref.at[phase, piece], chips - 1, recv_sem.at[sem(phase, piece, 1)])
 
         def body(k, total):
-            return total + recv_ref[phase, k].astype(F32)
-
-        total = lax.fori_loop(0, chips, body, jnp.zeros((block, width), F32))
+            return total + recv_ref[phase, piece, k].astype(F32)
+
+        total = lax.fori_loop(0, chips, body, jnp.zeros((block, wide), F32))
 
         def lines(part):
-            return jnp.concatenate(
-                [part[:, k : k + LANES] for k in range(0, width, LANES)], axis=0
-            )
+            return jnp.concatenate([part[:, k : k + LANES] for k in range(0, wide, LANES)], axis=0)
 
         return lines(total[:half]), lines(total[half:])
-
-    parts = width // LANES
 
     def unlines(part):
         return jnp.concatenate([part[k * half : (k + 1) * half] for k in range(parts)], axis=1)
@@ -334,14 +350,14 @@
         imaginary = jnp.concatenate([skew_ref[shift, half:]] * parts, axis=0)
         return real, imaginary
 
-    def all_gather(phase, ref):
+    def gather_push(ref, at):
         def push(k, carry):
             target = lax.rem(chip + k, chips)
             pltpu.make_async_remote_copy(
                 src_ref=ref.at[own],
                 dst_ref=ref.at[own],
-                send_sem=send_sem.at[4 * phase + 2],
-                recv_sem=recv_sem.at[4 * phase + 2],
+                send_sem=send_sem.at[at],
+                recv_sem=recv_sem.at[at],
                 device_id=place(target),
                 device_id_type=MESH,
             ).start()
@@ -349,17 +365,23 @@
 
         lax.fori_loop(1, chips, push, 0)
 
-    def all_gather_wait(phase, ref):
-        wait_owned(ref, recv_sem.at[4 * phase + 2])
-        pair = to_sibling(ref.at[mine], ref.at[mine], 4 * phase + 3)
-        pair.start()
-        pair.wait()
-        if_owner(
-            lambda: wait_chunks(ref.at[pl.ds(0, group)], chips - 1, send_sem.at[4 * phase + 2])
-        )
-        wait_owned(send_ref, send_sem.at[4 * phase + 1])
-
-    all_to_all(0, field_ref, fwd_ref)
+    def gather_pass(ref, at):
+        wait_owned(ref, recv_sem.at[at])
+        to_sibling(ref.at[mine], ref.at[mine], at + 1).start()
+
+    def gather_wait(ref, at):
+        to_sibling(ref.at[mine], ref.at[mine], at + 1).wait()
+
+    def gather_end(ref, at):
+        if_owner(lambda: wait_chunks(ref.at[pl.ds(0, group)], chips - 1, send_sem.at[at]))
+
+    give(0, 0, field_ref, fwd_ref)
+    keep(0, field_ref, fwd_ref)
+    give(0, 1, field_ref, fwd_ref)
+    send(0, 0)
+    keep(1, field_ref, fwd_ref)
+    send(0, 1)
+
     fill(1, inv_ref)
     step = mix_ref.shape[0]
     repeat = ones((step, C), lambda r, l: r % C == l)
@@ -385,11 +407,10 @@
         )
         skew_ref[shift] = dot(weight_ref[...], pick)
 
-    @if_owner
-    def _():
-        real, imaginary = all_to_all_sum(0)
-        coef_ref[0] = real
-        coef_ref[1] = imaginary
+    def mix(piece):
+        real, imaginary = collect(0, piece)
+        coef_ref[piece, 0] = real
+        coef_ref[piece, 1] = imaginary
         out_real = jnp.zeros_like(real)
         out_imag = jnp.zeros_like(real)
         for shift in range(C):
@@ -399,29 +420,43 @@
             out_real = out_real + (c_real * w_real - c_imag * w_imag)
             out_imag = out_imag + (c_real * w_imag + c_imag * w_real)
         mixed = jnp.concatenate([unlines(out_real), unlines(out_imag)], axis=0)
-        out_ref[own] = mixed.astype(BF16)
-        all_gather(0, out_ref)
-
-    all_gather_wait(0, out_ref)
+        out_ref[piece, own] = mixed.astype(BF16)
+        gather_push(out_ref.at[piece], sem(0, piece, 2))
+
+    for piece in range(HALVES):
+        if_owner(functools.partial(mix, piece))
 
     chunk = 4 * rows_y
-
-    def local(value, matrix):
-        return jnp.concatenate(
-            [dot(value[:, k : k + step], matrix) for k in range(0, width, step)], axis=1
-        )
-
-    def activate(index, carry):
+    steps = cells // chunk
+
+    def activate(piece, index, carry):
         here = pl.ds(pl.multiple_of(index * chunk, chunk), chunk)
-        spectral = dot(inv_ref[here, :], out_ref[...].reshape(columns, width))
-        preact = spectral.astype(BF16).astype(F32) + local(field_ref[here, :], mix_ref[...])
+        part = strip(piece)
+        spectral = dot(inv_ref[here, :], out_ref[piece].reshape(columns, wide))
+        preact = spectral.astype(BF16).astype(F32) + dot(field_ref[here, part], mix_ref[...])
         bell = 0.5 * (1.0 + lax.erf(preact * ROOT_HALF))
         tail = preact * jnp.exp(-0.5 * preact * preact) * INV_ROOT_TWO_PI
-        slope_ref[here, :] = (bell + tail) * proj_ref[...]
-        press_ref[here, :] = split_dot(preact * bell * proj_ref[...], sum_ref[...])
+        row_proj = proj_ref[:, part]
+        slope_ref[here, part] = (bell + tail) * row_proj
+        share = split_dot(preact * bell * row_proj, sum_ref[part, :])
+        press_ref[here, :] = share if piece == 0 else press_ref[here, :] + share
         return carry
 
-    lax.fori_loop(0, cells // chunk, activate, 0)
+    def staged(phase, ref, work):
+        gather_pass(ref.at[0], sem(phase, 0, 2))
+        gather_wait(ref.at[0], sem(phase, 0, 2))
+        lax.fori_loop(0, steps // 2, functools.partial(work, 0), 0)
+        gather_pass(ref.at[1], sem(phase, 1, 2))
+        lax.fori_loop(steps // 2, steps, functools.partial(work, 0), 0)
+        gather_wait(ref.at[1], sem(phase, 1, 2))
+        lax.fori_loop(0, steps, functools.partial(work, 1), 0)
+
+    def end_sends(phase, ref):
+        for piece in range(HALVES):
+            gather_end(ref.at[piece], sem(phase, piece, 2))
+            wait_owned(send_ref.at[piece], send_sem.at[sem(phase, piece, 1)])
+
+    staged(0, out_ref, activate)
 
     def gathered(index):
         made = press_ref[pl.ds(index * per, rows_x, stride=rows_y), :]
@@ -430,6 +465,7 @@
             made = jnp.where(lane // depth == k, other, made)
         return made
 
+    end_sends(0, out_ref)
     pressure = jnp.concatenate([gathered(k) for k in range(rows_y // per)], axis=1)
     halo_start(1, pressure)
     halo_wait(0)
@@ -454,29 +490,37 @@
                 lane // depth == j, piece, 0.0
             )
 
-    def differentiate(index, carry):
+    def differentiate(piece, index, carry):
         here = pl.ds(pl.multiple_of(index * chunk, chunk), chunk)
-        wide = split_dot(press_ref[here, :], spread_ref[...])
-        pre_ref[here, :] = (wide * slope_ref[here, :]).astype(BF16)
+        part = strip(piece)
+        source = split_dot(press_ref[here, :], spread_ref[:, part])
+        pre_ref[here, part] = (source * slope_ref[here, part]).astype(BF16)
         return carry
 
-    lax.fori_loop(0, cells // chunk, differentiate, 0)
-
-    all_to_all(1, pre_ref, inv_ref)
-
-    @if_owner
-    def _():
-        g_real, g_imag = all_to_all_sum(1)
-        real = coef_ref[0]
-        imaginary = coef_ref[1]
+    lax.fori_loop(0, steps, functools.partial(differentiate, 0), 0)
+    give(1, 0, pre_ref, inv_ref)
+    keep(0, pre_ref, inv_ref)
+    lax.fori_loop(0, steps, functools.partial(differentiate, 1), 0)
+    send(1, 0)
+    give(1, 1, pre_ref, inv_ref)
+    keep(1, pre_ref, inv_ref)
+    send(1, 1)
+
+    def mix_back(piece):
+        g_real, g_imag = collect(1, piece)
+        real = coef_ref[piece, 0]
+        imaginary = coef_ref[piece, 1]
         in_real = jnp.zeros_like(real)
         in_imag = jnp.zeros_like(real)
-        grads = [[jnp.zeros((half, LANES), F32) for _ in range(C * C // LANES)] for _ in range(2)]
-        spot = lane_iota((half, LANES))
         for shift in range(C):
             w_real, w_imag = weights(shift)
-            in_real = in_real + group_roll(g_real * w_real + g_imag * w_imag, (C - shift) % C)
-            in_imag = in_imag + group_roll(g_imag * w_real - g_real * w_imag, (C - shift) % C)
+            back = (C - shift) % C
+            in_real = in_real + group_roll(g_real * w_real + g_imag * w_imag, back)
+            in_imag = in_imag + group_roll(g_imag * w_real - g_real * w_imag, back)
+        mixed = jnp.concatenate([unlines(in_real), unlines(in_imag)], axis=0)
+        gout_ref[piece, own] = mixed.astype(BF16)
+        gather_push(gout_ref.at[piece], sem(1, piece, 2))
+        for shift in range(C):
             c_real = group_roll(real, shift)
             c_imag = group_roll(imaginary, shift)
             both = (c_real * g_real + c_imag * g_imag, c_real * g_imag - c_imag * g_real)
@@ -484,6 +528,17 @@
                 total = both[which][:half]
                 for k in range(1, parts):
                     total = total + both[which][k * half : (k + 1) * half]
+                if piece > 0:
+                    total = total + total_ref[which, shift]
+                total_ref[which, shift] = total
+
+    def weight_terms():
+        spot = lane_iota((half, LANES))
+        lines = []
+        for which in range(2):
+            grads = [jnp.zeros((half, LANES), F32) for _ in range(C * C // LANES)]
+            for shift in range(C):
+                total = total_ref[which, shift]
                 turn = C
                 while turn < LANES:
                     total = total + pltpu.roll(total, turn, 1)
@@ -491,30 +546,31 @@
                 for k in range(C * C // LANES):
                     source = k * (LANES // C) + spot // C
                     match = (spot % C - source + C) % C == shift
-                    grads[which][k] = jnp.where(match, total, grads[which][k])
-        message = jnp.concatenate(
-            [
-                jnp.concatenate([unlines(in_real)] + grads[0], axis=1),
-                jnp.concatenate([unlines(in_imag)] + grads[1], axis=1),
-            ],
-            axis=0,
-        )
-        gout_ref[own] = message.astype(BF16)
-        all_gather(1, gout_ref)
-
-    all_gather_wait(1, gout_ref)
-
-    def finish(index, carry):
+                    grads[k] = jnp.where(match, total, grads[k])
+            lines.append(jnp.concatenate(grads, axis=1))
+        terms_ref[own] = jnp.concatenate(lines, axis=0).astype(BF16)
+        gather_push(terms_ref, sem(2, 0, 0))
+
+    for piece in range(HALVES):
+        if_owner(functools.partial(mix_back, piece))
+    if_owner(weight_terms)
+
+    def finish(piece, index, carry):
         here = pl.ds(pl.multiple_of(index * chunk, chunk), chunk)
-        spectral = dot(fwd_ref[here, :], gout_ref[:, :, :width].reshape(columns, width))
-        total = spectral.astype(BF16).astype(F32) + local(pre_ref[here, :], mix_t_ref[...])
-        grad_ref[here, :] = total.astype(BF16)
+        part = strip(piece)
+        spectral = dot(fwd_ref[here, :], gout_ref[piece].reshape(columns, wide))
+        total = spectral.astype(BF16).astype(F32) + dot(pre_ref[here, part], mix_t_ref[...])
+        grad_ref[here, part] = total.astype(BF16)
         return carry
 
-    lax.fori_loop(0, cells // chunk, finish, 0)
+    staged(1, gout_ref, finish)
+    gather_pass(terms_ref, sem(2, 0, 0))
+    end_sends(1, gout_ref)
+    gather_wait(terms_ref, sem(2, 0, 0))
+    gather_end(terms_ref, sem(2, 0, 0))
 
     def report(k, carry):
-        terms = gout_ref[k, :, width:].astype(F32)
+        terms = terms_ref[k].astype(F32)
         spec_ref[0, k] = terms[:half]
         spec_ref[1, k] = terms[half:]
         return carry
@@ -567,7 +623,8 @@
     weights = lax.dynamic_slice_in_dim(
         spec_weight.reshape(2, KX * KY, C, C), own * modes, modes, 1
     ).reshape(block, C * C)
-    step = min(256, width)
+    wide = width // HALVES
+    step = wide
 
     vmem = pl.BlockSpec(memory_space=pltpu.VMEM)
     smem = pl.BlockSpec(memory_space=pltpu.SMEM)
@@ -583,16 +640,18 @@
         scratch_shapes=[
             pltpu.VMEM((cells, columns), BF16),
             pltpu.VMEM((cells, columns), BF16),
-            pltpu.VMEM((owners, block, width), BF16),
-            pltpu.VMEM((2, n // 2, block, width), BF16),
-            pltpu.VMEM((owners, block, width), BF16),
-            pltpu.VMEM((owners, block, width + C * C), BF16),
+            pltpu.VMEM((HALVES, owners, block, wide), BF16),
+            pltpu.VMEM((2, HALVES, n // 2, block, wide), BF16),
+            pltpu.VMEM((HALVES, owners, block, wide), BF16),
+            pltpu.VMEM((HALVES, owners, block, wide), BF16),
+            pltpu.VMEM((owners, block, C * C), BF16),
+            pltpu.VMEM((2, C, modes, LANES), F32),
             pltpu.VMEM((cells, width), F32),
             pltpu.VMEM((cells, width), BF16),
             pltpu.VMEM((cells, LANES), F32),
-            pltpu.VMEM((2, modes * width // LANES, LANES), F32),
-            pltpu.VMEM((2, owners // 2, block, width), BF16),
-            pltpu.VMEM((columns // 2, width), F32),
+            pltpu.VMEM((HALVES, 2, modes * wide // LANES, LANES), F32),
+            pltpu.VMEM((2, HALVES, owners // 2, block, wide), BF16),
+            pltpu.VMEM((HALVES, columns // 2, wide), F32),
             pltpu.VMEM((C, block, LANES), F32),
             pltpu.VMEM((step, step), BF16),
             pltpu.VMEM((step, step), BF16),
@@ -603,8 +662,8 @@
             pltpu.VMEM((3, 2, 1, rows_y * depth), F32),
             pltpu.VMEM((3, 2, rows_x, LANES), F32),
             pltpu.VMEM((3, 2, rows_x, LANES), F32),
-            pltpu.SemaphoreType.DMA((8,)),
-            pltpu.SemaphoreType.DMA((8,)),
+            pltpu.SemaphoreType.DMA((18,)),
+            pltpu.SemaphoreType.DMA((18,)),
             pltpu.SemaphoreType.DMA((3, 4)),
             pltpu.SemaphoreType.DMA((3, 4)),
         ],

time: 83.3 us -> 76 us (0.912)
  Pallas kernels: 72.2 us -> 64.8 us
    pallas_call x1, Pallas kernels: 72.2 us -> 64.8 us  [shards(): pl.pallas_call(functools.partial(kernel, gxn, gyn, owners, rows_x, rows_y...]
where the time goes in v3:
time: 76 us; the launch traced here: 75.3 us
  Pallas kernels  64.8 us (85%)
  local copies, waits for them, and re-layouts  9.85 us (13%)
    pallas_call x1, Pallas kernels, shards(): pl.pallas_call(functools.partial(kernel, gxn, gyn, owners, rows_x, rows_y...  64.8 us
    unnamed x6, local copies, waits for them, and re-layouts  5.4 us
    reshape x1, local copies, waits for them, and re-layouts, shards(): spec_grad = spec.reshape(2, KX, KY, C, C)  3.73 us

profile of v3, /device:TPU:0, one launch (start us, length us, event | category | flops | bytes accessed | tf_op | source)
XLA Modules:
  0.0 75.3 jit_solution(17436233205713657900)
XLA Ops:
  0.6 0.0 copy-start
  0.7 1.6 %copy-done = bf16[2,16,16,16,16]{4,3,2,1,0:T(8,128)(2,1)S(1)} copy-done((bf16[2,16,16,16,16]{4,3,2,1,0:T(8,128)(2,1)S(1)}, bf16[2,16,16,16,16]{4,3,2,1,0:T(8,128)(2,1)}, u32[]{:S(2)}) %copy-start) | copy-done | bytes 262168
  2.2 0.7 reshape.23.weight_ref
  3.0 64.8 %fourier_darcy.1 = (f32[32,2048]{1,0:T(8,128)}, bf16[2048,512]{1,0:T(8,128)(2,1)}, f32[2,32,8,256]{3,2,1,0:T(8,128)}) custom-call(bf16[2048,512]{1,0:T(8,128)(2,1)} %bitcast.8, s32[32,2048]{1,0:T(8,128)} %class_ref.1, f32[8]{0:T(128)} %table_ref.1, f32[32,2048]{1,0:T(8,128)} %forcing_ref.1, bf16[512,128]{1,0:T(8,128)(2,1)} %constant.52.clone.x_ref, ...), custom_call_target="tpu_custom_call" | custom-call | tf_op jit(solution)/shard_map/fourier_darcy/pallas_call | solution.py:631
  67.8 0.0 copy-start.1
  67.8 3.7 %reshape.25 = f32[2,16,16,16,16]{4,3,2,1,0:T(8,128)} reshape(f32[2,32,8,256]{3,2,1,0:T(8,128)} %get-tuple-element.8) | data formatting | bytes 1048576 | tf_op jit(solution)/shard_map/reshape | solution.py:685
  71.5 0.0 copy-done.1
  71.5 0.7 copy.14
  72.2 3.1 %copy.15 = bf16[32,64,512]{2,1,0:T(8,128)(2,1)} copy(bf16[32,64,512]{2,1,0:T(8,128)(2,1)} %bitcast.9) | data formatting | bytes 4194304
  (1 shorter events, 0.0 us)
Async XLA Ops:
  0.6 1.6 %copy-start = (bf16[2,16,16,16,16]{4,3,2,1,0:T(8,128)(2,1)S(1)}, bf16[2,16,16,16,16]{4,3,2,1,0:T(8,128)(2,1)}, u32[]{:S(2)}) copy-start(bf16[2,16,16,16,16]{4,3,2,1,0:T(8,128)(2,1)} %param.13) | copy-start | bytes 786436
  67.8 3.7 %copy-start.1 = (f32[32,2048]{1,0:T(8,128)S(1)}, f32[32,2048]{1,0:T(8,128)}, u32[]{:S(2)}) copy-start(f32[32,2048]{1,0:T(8,128)} %get-tuple-element.12) | copy-start | bytes 786436

commit v4 on v3

--- a/solution.py
+++ b/solution.py
@@ -56,7 +56,7 @@
     rows_x,
     rows_y,
     depth,
-    field_ref,
+    field_in,
     class_ref,
     table_ref,
     forcing_ref,
@@ -68,6 +68,10 @@
     residual_ref,
     grad_ref,
     spec_ref,
+    field_ref,
+    bell_ref,
+    applied_ref,
+    load_sem,
     fwd_ref,
     inv_ref,
     send_ref,
@@ -126,6 +130,8 @@
     def place(index):
         return (2 * (index // gyn) + core, index % gyn)
 
+    load = pltpu.make_async_copy(field_in, field_ref, load_sem)
+    load.start()
     sibling = (gx + 1 - 2 * core, gy)
     beside = gx - 1 + 2 * core
     has_beside = jnp.logical_and(beside >= 0, beside < gxn)
@@ -232,6 +238,7 @@
 
     row = lax.broadcasted_iota(jnp.int32, (rows_x, span), 0)
     layer = lane_iota((rows_x, span)) % depth
+    column_at = lane_iota((rows_x, span))
     lane = lane_iota((rows_x, LANES))
 
     def neighbours(turn, value):
@@ -375,6 +382,7 @@
     def gather_end(ref, at):
         if_owner(lambda: wait_chunks(ref.at[pl.ds(0, group)], chips - 1, send_sem.at[at]))
 
+    load.wait()
     give(0, 0, field_ref, fwd_ref)
     keep(0, field_ref, fwd_ref)
     give(0, 1, field_ref, fwd_ref)
@@ -435,9 +443,9 @@
         spectral = dot(inv_ref[here, :], out_ref[piece].reshape(columns, wide))
         preact = spectral.astype(BF16).astype(F32) + dot(field_ref[here, part], mix_ref[...])
         bell = 0.5 * (1.0 + lax.erf(preact * ROOT_HALF))
-        tail = preact * jnp.exp(-0.5 * preact * preact) * INV_ROOT_TWO_PI
         row_proj = proj_ref[:, part]
-        slope_ref[here, part] = (bell + tail) * row_proj
+        slope_ref[here, part] = preact
+        bell_ref[here, part] = bell
         share = split_dot(preact * bell * row_proj, sum_ref[part, :])
         press_ref[here, :] = share if piece == 0 else press_ref[here, :] + share
         return carry
@@ -468,21 +476,54 @@
     end_sends(0, out_ref)
     pressure = jnp.concatenate([gathered(k) for k in range(rows_y // per)], axis=1)
     halo_start(1, pressure)
+
+    def slope(piece, index, carry):
+        here = pl.ds(pl.multiple_of(index * chunk, chunk), chunk)
+        part = strip(piece)
+        preact = slope_ref[here, part]
+        tail = preact * jnp.exp(-0.5 * preact * preact) * INV_ROOT_TWO_PI
+        slope_ref[here, part] = (bell_ref[here, part] + tail) * proj_ref[:, part]
+        return carry
+
     halo_wait(0)
     means = [0.5 * (perm + other) for other in neighbours(0, perm)]
+
+    def operator_inside(value):
+        def term(mean, axis, amount, outside):
+            made = mean * (value - pltpu.roll(value, amount, axis))
+            return jnp.where(outside, 0.0, made)
+
+        total = means[4] * (value - jnp.where(layer == 0, 0.0, pltpu.roll(value, 1, 1)))
+        total = total + means[5] * (
+            value - jnp.where(layer == depth - 1, 0.0, pltpu.roll(value, span - 1, 1))
+        )
+        total = total + term(means[0], 0, 1, row == 0)
+        total = total + term(means[1], 0, rows_x - 1, row == rows_x - 1)
+        total = total + term(means[2], 1, depth, column_at < depth)
+        return total + term(means[3], 1, span - depth, column_at >= span - depth)
+
+    def operator_faces(turn, value, ref):
+        last = rows_x - 1
+        ref[0:1, :] += means[0][0:1] * (value[0:1] - x_recv[turn, 0])
+        ref[last : last + 1, :] += means[1][last:] * (value[last:] - x_recv[turn, 1])
+        other = pltpu.roll(y_recv[turn, 0], depth, 1)
+        made = means[2][:, :LANES] * (value[:, :LANES] - other)
+        ref[:, :LANES] += jnp.where(lane < depth, made, 0.0)
+        other = pltpu.roll(y_recv[turn, 1], LANES - depth, 1)
+        made = means[3][:, span - LANES :] * (value[:, span - LANES :] - other)
+        ref[:, span - LANES :] += jnp.where(lane >= LANES - depth, made, 0.0)
+
+    residual_ref[...] = operator_inside(pressure) - forcing_ref[...]
+    lax.fori_loop(0, steps, functools.partial(slope, 0), 0)
     halo_wait(1)
-
-    def operator(turn, value):
-        total = jnp.zeros_like(value)
-        for mean, other in zip(means, neighbours(turn, value)):
-            total = total + mean * (value - other)
-        return total
-
-    residual = operator(1, pressure) - forcing_ref[...]
-    residual_ref[...] = residual
+    operator_faces(1, pressure, residual_ref)
+    residual = residual_ref[...]
     halo_start(2, residual)
+    applied_ref[...] = operator_inside(residual)
+    lax.fori_loop(0, steps, functools.partial(slope, 1), 0)
     halo_wait(2)
-    slope_source = operator(2, residual)
+    operator_faces(2, residual, applied_ref)
+    slope_source = applied_ref[...]
     for k in range(rows_y // per):
         piece = slope_source[:, k * LANES : (k + 1) * LANES]
         for j in range(per):
@@ -635,9 +676,13 @@
             jax.ShapeDtypeStruct((cells, width), BF16),
             jax.ShapeDtypeStruct((2, owners, modes, C * C), F32),
         ),
-        in_specs=[vmem, vmem, smem] + [vmem] * 5 + [smem],
+        in_specs=[pl.BlockSpec(memory_space=pl.ANY), vmem, smem] + [vmem] * 5 + [smem],
         out_specs=(vmem, vmem, vmem),
         scratch_shapes=[
+            pltpu.VMEM((cells, width), BF16),
+            pltpu.VMEM((cells, width), F32),
+            pltpu.VMEM((rows_x, rows_y * depth), F32),
+            pltpu.SemaphoreType.DMA,
             pltpu.VMEM((cells, columns), BF16),
             pltpu.VMEM((cells, columns), BF16),
             pltpu.VMEM((HALVES, owners, block, wide), BF16),

time: 76 us -> 74.3 us (0.978)
  Pallas kernels: 64.8 us -> 63.5 us
    pallas_call x1, Pallas kernels: 64.8 us -> 63.5 us  [shards(): pl.pallas_call(functools.partial(kernel, gxn, gyn, owners, rows_x, rows_y...]
where the time goes in v4:
time: 74.3 us; the launch traced here: 74 us
  Pallas kernels  63.5 us (85%)
  local copies, waits for them, and re-layouts  9.85 us (13%)
    pallas_call x1, Pallas kernels, shards(): pl.pallas_call(functools.partial(kernel, gxn, gyn, owners, rows_x, rows_y...  63.5 us
    unnamed x6, local copies, waits for them, and re-layouts  5.4 us
    reshape x1, local copies, waits for them, and re-layouts, shards(): spec_grad = spec.reshape(2, KX, KY, C, C)  3.73 us

profile of v4, /device:TPU:0, one launch (start us, length us, event | category | flops | bytes accessed | tf_op | source)
XLA Modules:
  0.0 74.0 jit_solution(12330179007000733965)
XLA Ops:
  0.6 0.0 copy-start
  0.7 1.6 %copy-done = bf16[2,16,16,16,16]{4,3,2,1,0:T(8,128)(2,1)S(1)} copy-done((bf16[2,16,16,16,16]{4,3,2,1,0:T(8,128)(2,1)S(1)}, bf16[2,16,16,16,16]{4,3,2,1,0:T(8,128)(2,1)}, u32[]{:S(2)}) %copy-start) | copy-done | bytes 262168
  2.2 0.7 reshape.23.weight_ref
  3.0 63.5 %fourier_darcy.1 = (f32[32,2048]{1,0:T(8,128)}, bf16[2048,512]{1,0:T(8,128)(2,1)}, f32[2,32,8,256]{3,2,1,0:T(8,128)}) custom-call(bf16[2048,512]{1,0:T(8,128)(2,1)} %bitcast.8, s32[32,2048]{1,0:T(8,128)} %class_ref.1, f32[8]{0:T(128)} %table_ref.1, f32[32,2048]{1,0:T(8,128)} %forcing_ref.1, bf16[512,128]{1,0:T(8,128)(2,1)} %constant.52.clone.x_ref, ...), custom_call_target="tpu_custom_call" | custom-call | tf_op jit(solution)/shard_map/fourier_darcy/pallas_call | solution.py:672
  66.5 0.0 copy-start.1
  66.5 3.7 %reshape.25 = f32[2,16,16,16,16]{4,3,2,1,0:T(8,128)} reshape(f32[2,32,8,256]{3,2,1,0:T(8,128)} %get-tuple-element.8) | data formatting | bytes 1048576 | tf_op jit(solution)/shard_map/reshape | solution.py:730
  70.2 0.0 copy-done.1
  70.2 0.7 copy.14
  70.9 3.1 %copy.15 = bf16[32,64,512]{2,1,0:T(8,128)(2,1)} copy(bf16[32,64,512]{2,1,0:T(8,128)(2,1)} %bitcast.9) | data formatting | bytes 4194304
  (1 shorter events, 0.0 us)
Async XLA Ops:
  0.6 1.6 %copy-start = (bf16[2,16,16,16,16]{4,3,2,1,0:T(8,128)(2,1)S(1)}, bf16[2,16,16,16,16]{4,3,2,1,0:T(8,128)(2,1)}, u32[]{:S(2)}) copy-start(bf16[2,16,16,16,16]{4,3,2,1,0:T(8,128)(2,1)} %param.13) | copy-start | bytes 786436
  66.5 3.7 %copy-start.1 = (f32[32,2048]{1,0:T(8,128)S(1)}, f32[32,2048]{1,0:T(8,128)}, u32[]{:S(2)}) copy-start(f32[32,2048]{1,0:T(8,128)} %get-tuple-element.12) | copy-start | bytes 786436

commit v5 on v4

--- a/solution.py
+++ b/solution.py
@@ -66,8 +66,10 @@
     mixing_ref,
     proj_in,
     residual_ref,
+    grad_out,
+    spec_ref,
     grad_ref,
-    spec_ref,
+    store_sem,
     field_ref,
     bell_ref,
     applied_ref,
@@ -602,6 +604,8 @@
         spectral = dot(fwd_ref[here, :], gout_ref[piece].reshape(columns, wide))
         total = spectral.astype(BF16).astype(F32) + dot(pre_ref[here, part], mix_t_ref[...])
         grad_ref[here, part] = total.astype(BF16)
+        if piece == HALVES - 1:
+            pltpu.make_async_copy(grad_ref.at[here], grad_out.at[here], store_sem).start()
         return carry
 
     staged(1, gout_ref, finish)
@@ -617,6 +621,7 @@
         return carry
 
     lax.fori_loop(0, owners, report, 0)
+    pltpu.make_async_copy(grad_ref, grad_out, store_sem).wait()
 
 
 def angle_tables(length, count, scale):
@@ -677,8 +682,10 @@
             jax.ShapeDtypeStruct((2, owners, modes, C * C), F32),
         ),
         in_specs=[pl.BlockSpec(memory_space=pl.ANY), vmem, smem] + [vmem] * 5 + [smem],
-        out_specs=(vmem, vmem, vmem),
+        out_specs=(vmem, pl.BlockSpec(memory_space=pl.ANY), vmem),
         scratch_shapes=[
+            pltpu.VMEM((cells, width), BF16),
+            pltpu.SemaphoreType.DMA,
             pltpu.VMEM((cells, width), BF16),
             pltpu.VMEM((cells, width), F32),
             pltpu.VMEM((rows_x, rows_y * depth), F32),

time: 74.3 us -> 73.6 us (level)
  no operation moved by 1% of the time
where the time goes in v5:
time: 73.6 us; the launch traced here: 73.4 us
  Pallas kernels  62.8 us (85%)
  local copies, waits for them, and re-layouts  9.85 us (13%)
    pallas_call x1, Pallas kernels, shards(): pl.pallas_call(functools.partial(kernel, gxn, gyn, owners, rows_x, rows_y...  62.8 us
    unnamed x6, local copies, waits for them, and re-layouts  5.4 us
    reshape x1, local copies, waits for them, and re-layouts, shards(): spec_grad = spec.reshape(2, KX, KY, C, C)  3.73 us

profile of v5, /device:TPU:0, one launch (start us, length us, event | category | flops | bytes accessed | tf_op | source)
XLA Modules:
  0.0 73.4 jit_solution(15840070292280673459)
XLA Ops:
  0.6 0.0 copy-start
  0.7 1.6 %copy-done = bf16[2,16,16,16,16]{4,3,2,1,0:T(8,128)(2,1)S(1)} copy-done((bf16[2,16,16,16,16]{4,3,2,1,0:T(8,128)(2,1)S(1)}, bf16[2,16,16,16,16]{4,3,2,1,0:T(8,128)(2,1)}, u32[]{:S(2)}) %copy-start) | copy-done | bytes 262168
  2.2 0.7 reshape.23.weight_ref
  3.0 62.8 %fourier_darcy.1 = (f32[32,2048]{1,0:T(8,128)}, bf16[2048,512]{1,0:T(8,128)(2,1)}, f32[2,32,8,256]{3,2,1,0:T(8,128)}) custom-call(bf16[2048,512]{1,0:T(8,128)(2,1)} %bitcast.8, s32[32,2048]{1,0:T(8,128)} %class_ref.1, f32[8]{0:T(128)} %table_ref.1, f32[32,2048]{1,0:T(8,128)} %forcing_ref.1, bf16[512,128]{1,0:T(8,128)(2,1)} %constant.52.clone.x_ref, ...), custom_call_target="tpu_custom_call" | custom-call | tf_op jit(solution)/shard_map/fourier_darcy/pallas_call | solution.py:677
  65.8 0.0 copy-start.1
  65.8 3.7 %reshape.25 = f32[2,16,16,16,16]{4,3,2,1,0:T(8,128)} reshape(f32[2,32,8,256]{3,2,1,0:T(8,128)} %get-tuple-element.8) | data formatting | bytes 1048576 | tf_op jit(solution)/shard_map/reshape | solution.py:737
  69.5 0.0 copy-done.1
  69.5 0.7 copy.14
  70.2 3.1 %copy.15 = bf16[32,64,512]{2,1,0:T(8,128)(2,1)} copy(bf16[32,64,512]{2,1,0:T(8,128)(2,1)} %bitcast.9) | data formatting | bytes 4194304
  (1 shorter events, 0.0 us)
Async XLA Ops:
  0.6 1.6 %copy-start = (bf16[2,16,16,16,16]{4,3,2,1,0:T(8,128)(2,1)S(1)}, bf16[2,16,16,16,16]{4,3,2,1,0:T(8,128)(2,1)}, u32[]{:S(2)}) copy-start(bf16[2,16,16,16,16]{4,3,2,1,0:T(8,128)(2,1)} %param.13) | copy-start | bytes 786436
  65.8 3.7 %copy-start.1 = (f32[32,2048]{1,0:T(8,128)S(1)}, f32[32,2048]{1,0:T(8,128)}, u32[]{:S(2)}) copy-start(f32[32,2048]{1,0:T(8,128)} %get-tuple-element.12) | copy-start | bytes 786436
